TPU v7x, 32 devices: a whole 2x2x4 slice. The times are simulated.
32 devices in a mesh: rep: 16 (over z, x, core), head: 2 (over y).
Axes of the slice: x: 2, y: 2, z: 4, core: 2. Of those that a mesh axis runs over, the one named last changes fastest.
Arguments:
- states: float32 [32, 8, 128, 128], P('rep', 'head'), may hold values from -4 to 4
- conv_states: bfloat16 [32, 3, 3, 1024], P('rep', None, None, 'head'), may hold values from -6 to 6
- projected: bfloat16 [6, 32, 3, 1024], P(None, 'rep', None, 'head'), may hold values from -6 to 6
- conv_weight: float32 [4, 3, 1024], P(None, None, 'head'), may hold values from -3 to 3
- decay_input: float32 [6, 32, 1024], P(None, 'rep', 'head'), may hold values from -6 to 6
- decay_rate: float32 [8], P('head'), may hold values from 0.05 to 2
- beta_logit: float32 [6, 32, 8], P(None, 'rep', 'head'), may hold values from -6 to 6
- out_gate: bfloat16 [6, 32, 1024], P(None, 'rep', 'head'), may hold values from -6 to 6
- norm_gain: float32 [128], replicated, may hold values from 0.25 to 1.75
- out_weight: bfloat16 [1024, 2304], P('head'), may hold values from -0.25 to 0.25
- destinations: int32 [6, 32], replicated, may hold values from 0 to 31, as said below
- live_counts: int32 [6, 16], P(None, 'rep'), may hold values from 1 to 2
Outputs:
- layer_out: bfloat16 [6, 32, 2304], P(None, 'rep', 'head')
- states_out: float32 [32, 8, 128, 128], P('rep', 'head')
- conv_out: bfloat16 [32, 3, 3, 1024], P('rep', None, None, 'head')
Inputs may be any that keep to these rules, and one draw needn't show every extreme that they name: For each step t, destinations[t] is a permutation of the 32 slots; slot g belongs to replica group g // 2. In every step, the number of slots g of each group with destinations[t, g] != g is exactly 1.
All inputs are finite; a program needn't handle non-finite values.
Results may differ from a plain program's by a relative error of at most 0.015.
Values may be sent and summed in bfloat16 or wider, within the bound.
No kernel may reach another device: no remote copies, remote signals or barrier semaphores. Data moves between devices by JAX's collectives and lax.ppermute only.
A program may use at most 128 MiB of HBM per device.

v0:
```python
import functools

import jax
import jax.numpy as jnp
from jax import lax
from jax.experimental import pallas as pl
from jax.experimental.pallas import tpu as pltpu
from jax.sharding import PartitionSpec as P

EPSILON = 1e-06
LANES = 128
VMEM_LIMIT = 32 * 1024 * 1024
F32 = jnp.float32
BF16 = jnp.bfloat16


def round_up(value, multiple):
    return -(-value // multiple) * multiple


class Sizes:
    def __init__(self, group_total, states, conv_states, projected):
        self.groups = n = group_total
        self.rows, self.heads, self.dk, _ = states.shape
        self.taps, self.parts = conv_states.shape[1:3]
        self.steps = projected.shape[0]
        self.slots = n * self.rows
        self.cuts = n // self.heads
        far = [*range(0, self.heads, 2), *range(1, self.heads, 2)]
        self.order = [h * self.cuts + cut for cut in range(self.cuts) for h in far]
        self.place_of = [self.order.index(p) for p in range(n)]
        self.cols = self.dk // self.cuts
        self.state_rows = self.rows * self.cols
        self.quarter = self.dk // 4
        self.decay_at = self.steps * 2 * self.rows
        self.hist_at = self.decay_at + self.steps * self.rows
        self.value_at = self.hist_at + self.taps * 2 * self.rows
        self.value_depth = -(-(self.steps + self.taps) // 4)
        self.flag_at = self.value_depth * self.rows
        self.tail_rows = round_up(self.flag_at + self.rows, 8)
        self.info_rows = self.value_at + self.tail_rows
        self.back_sets = self.steps + self.taps * self.parts
        self.back_depth = -(-self.back_sets // 4)
        self.back_rows = round_up(self.back_depth * self.rows, 8)
        self.whole_tiles = self.cols % 16 == 0
        self.width = max(LANES, 8 * self.cols)
        self.tile = self.width // self.cols


def mod(value, size):
    return value & (size - 1) if size & (size - 1) == 0 else lax.rem(value, size)


def quotient(value, size):
    if size & (size - 1) == 0:
        return lax.shift_right_logical(value, jnp.int32(size.bit_length() - 1))
    return lax.div(value, jnp.int32(size))


def in_block(sz, shape, cut, shift):
    start = cut * sz.cols + shift * sz.quarter
    return mod(iota(shape, len(shape) - 1) + (2 * sz.dk - start), sz.dk) < sz.cols


def iota(shape, dim):
    return lax.broadcasted_iota(jnp.int32, shape, dim)


def one_hot(condition):
    return jnp.where(condition, 1.0, 0.0).astype(BF16)


def dot(lhs, rhs, lhs_dim=1, rhs_dim=0):
    return lax.dot_general(
        lhs, rhs, (((lhs_dim,), (rhs_dim,)), ((), ())), preferred_element_type=F32
    )


def pack_kernel(sz, *refs):
    count = 8
    sources, states_hbm = refs[:count], refs[count]
    pieces, pick, place, final, taps = refs[count + 1 : count + 6]
    scratch = refs[count + 6 :]
    targets, live, rate, beta, proj, hist, decay, filters, states = scratch[: count + 1]
    info, tails, strengths, in_sems = scratch[count + 1 :]
    copies = []

    def start(source, target):
        copies.append(pltpu.make_async_copy(source, target, in_sems.at[len(copies)]))
        copies[-1].start()

    for source, target in zip(sources, scratch):
        start(source, target)
    for r in range(sz.rows):
        for h in range(sz.heads):
            start(states_hbm.at[r, h], states.at[r, h])
    for copy in copies:
        copy.wait()
    route(sz, targets, pick, place, final)
    own_head = lax.axis_index("rep") // sz.cuts
    head_lanes = pl.ds(pl.multiple_of(own_head * sz.dk, sz.dk), sz.dk)
    for part in range(sz.parts):
        taps[part] = filters[part, :, head_lanes]
    channels, dk = sz.heads * sz.dk, sz.dk
    lane_head = quotient(iota((1, channels), 1), dk)
    rates = jnp.zeros((1, channels), F32)
    for h in range(sz.heads):
        rates = jnp.where(lane_head == h, rate[:, h : h + 1], rates)
    row_ids = iota((sz.rows, channels), 0)

    def keep(target, at, value):
        for h in range(sz.heads):
            target[h, at : at + sz.rows, :] = value[:, h * dk : (h + 1) * dk]

    tails[...] = jnp.zeros(tails.shape, F32)

    def keep_value(index, value):
        shift = index // sz.value_depth
        at = index % sz.value_depth * sz.rows
        for h in range(sz.heads):
            own = value[:, h * dk : (h + 1) * dk]
            if shift:
                own = pltpu.roll(own, shift * sz.quarter, 1)
            tails[shift, h, at : at + sz.rows, :] = own

    for t in range(sz.steps):
        for part in range(2):
            keep(info, (t * 2 + part) * sz.rows, proj[t, part].astype(F32))
        keep_value(t, proj[t, 2].astype(F32))
        x = decay[t]
        softplus = jnp.maximum(x, 0.0) + jnp.log1p(jnp.exp(-jnp.abs(x)))
        keep(
            info,
            sz.decay_at + t * sz.rows,
            jnp.where(row_ids < live[:, t : t + 1], rates * softplus, 0.0),
        )
    for tap in range(sz.taps):
        for part in range(2):
            keep(info, sz.hist_at + (tap * 2 + part) * sz.rows, hist[tap, part].astype(F32))
        keep_value(sz.steps + tap, hist[tap, 2].astype(F32))
    lane = iota((sz.heads, dk), 1)
    strengths[...] = jnp.zeros(strengths.shape, F32)
    for r in range(sz.rows):
        strengths[:, : sz.steps] = beta[r]
        lives = jnp.zeros((sz.heads, dk), F32)
        for t in range(sz.steps):
            lives = jnp.where((lane == t) & (r < live[:, t : t + 1]), 1.0, lives)
        strength = lives / (1.0 + jnp.exp(-strengths[...]))
        high = strength.astype(BF16).astype(F32)
        flags = high + pltpu.roll(lives, 16, 1) + pltpu.roll(strength - high, 32, 1)
        for h in range(sz.heads):
            at = sz.flag_at + r
            for shift in range(4):
                tails[shift, h, at : at + 1, :] = flags[h : h + 1]
    blocks = [
        [in_block(sz, (sz.tail_rows, dk), cut, shift) for shift in range(1, 4)]
        for cut in range(sz.cuts)
    ]
    for h in range(sz.heads):
        head = info[h].astype(BF16)
        across = [states[r, h].T for r in range(sz.rows)]
        for cut in range(sz.cuts):
            p, at = h * sz.cuts + cut, cut * sz.cols
            own = [a[at : at + sz.cols] for a in across]
            pieces[p, : sz.state_rows, :] = jnp.concatenate(own, axis=0).astype(BF16)
            pieces[p, sz.state_rows : sz.state_rows + sz.value_at, :] = head
            tail = tails[0, h]
            for shift in range(1, 4):
                tail = jnp.where(blocks[cut][shift - 1], tails[shift, h], tail)
            pieces[p, sz.state_rows + sz.value_at :, :] = tail.astype(BF16)


def route(sz, targets, pick, place, final):
    n, T = sz.slots, sz.steps

    def label(slot):
        return mod(slot, sz.rows) * sz.groups + quotient(slot, sz.rows)

    to_label = one_hot(label(iota((n, n), 0)) == iota((n, n), 1))
    ordered = dot(targets[...].astype(F32).astype(BF16), to_label)
    ordered = label((ordered + 0.5).astype(jnp.int32))
    steps = [one_hot(iota((n, n), 0) == ordered[t : t + 1]) for t in range(T)]
    chain = [steps[0]]
    for t in range(1, T):
        if t % 2:
            pair = dot(steps[t], steps[t - 1]).astype(BF16)
            chain.append(dot(pair, chain[t - 2]).astype(BF16) if t > 1 else pair)
        else:
            chain.append(dot(steps[t], chain[t - 1]).astype(BF16))
    for t in range(T):
        place[t] = chain[t]
        pick[t] = chain[t].astype(F32).T.astype(BF16)
    slot = iota((8, n), 1)
    row, group = quotient(slot, sz.groups), mod(slot, sz.groups)
    head, cut = quotient(group, sz.cuts), mod(group, sz.cuts)
    far = quotient(head, 2) + mod(head, 2) * ((sz.heads + 1) // 2)
    weights = (cut * sz.heads + far) * sz.rows + row
    places = dot(weights.astype(F32).astype(BF16), chain[T - 1])
    final[...] = (places + 0.5).astype(jnp.int32)


def gate_factor(sz, live, gain, gate, factor):
    channels = sz.heads * sz.dk
    gains = jnp.concatenate([gain[...]] * sz.heads, axis=1)
    row = iota((sz.rows, channels), 0)
    factor[...] = jnp.zeros(factor.shape, F32)
    for t in range(sz.steps):
        gates = gains / (1.0 + jnp.exp(-gate[t].astype(F32)))
        factor[t * sz.rows : (t + 1) * sz.rows, :] = jnp.where(
            row < live[:, t : t + 1], gates, 0.0
        )


def step_kernel(sz, filters, pick, place, came, *refs):
    count = sz.groups
    sources, sent, factor, scratch = refs[:4], refs[4], refs[5], refs[6:]
    scalars, live, gain, gate, info, later, back, sems = scratch
    copies = []
    for i, (source, target) in enumerate(zip(sources, scratch)):
        copies.append(pltpu.make_async_copy(source, target, sems.at[i]))
        copies[-1].start()
    n, dk, T = sz.slots, sz.dk, sz.steps
    mine = lax.axis_index("rep")
    cut = lax.rem(mine, sz.cuts)
    stride = sz.info_rows
    for g in range(count):
        info[g * stride : (g + 1) * stride, :] = came[g, sz.state_rows :, :].astype(F32)

    def gather(at):
        return jnp.concatenate(
            [info[pl.ds(at + r, count, stride=stride), :] for r in range(sz.rows)], axis=0
        )

    def gather_value(index):
        value = gather(sz.value_at + index % sz.value_depth * sz.rows)
        shift = index // sz.value_depth
        return pltpu.roll(value, sz.dk - shift * sz.quarter, 1) if shift else value

    weights = [filters[part] for part in range(sz.parts)]
    flags = gather(sz.value_at + sz.flag_at)
    window = [
        [gather(sz.hist_at + (tap * 2 + part) * sz.rows) for part in range(2)]
        + [gather_value(T + tap)]
        for tap in range(sz.taps)
    ]
    reach = jnp.ones((n, dk), F32)
    keys = []
    from_state, values, strengths, key_mix, read_mix = [], [], [], [], []
    for t in range(T):
        slots = [gather((t * 2 + part) * sz.rows) for part in range(2)]
        slots += [gather_value(t), gather(sz.decay_at + t * sz.rows), flags]
        moved = dot(pick[t], jnp.concatenate(slots, axis=1).astype(BF16))
        inputs = [moved[:, i * dk : (i + 1) * dk] for i in range(sz.parts + 2)]
        moved_flags = inputs[sz.parts + 1]
        strength = moved_flags[:, t : t + 1] + moved_flags[:, 32 + t : 33 + t]
        alive = moved_flags[:, 16 + t : 17 + t] > 0.5
        active = []
        for part in range(sz.parts):
            frames = [window[tap][part] for tap in range(sz.taps)] + [inputs[part]]
            total = frames[0] * weights[part][:1]
            for j in range(1, sz.taps + 1):
                total = total + frames[j] * weights[part][j : j + 1]
            active.append(total / (1.0 + jnp.exp(-total)))
            for tap in range(sz.taps):
                window[tap][part] = jnp.where(alive, frames[tap + 1], frames[tap])
        query, key = (
            x * lax.rsqrt(jnp.sum(x * x, axis=1, keepdims=True) + EPSILON) for x in active[:2]
        )
        retain = jnp.exp(-inputs[sz.parts])
        reach = reach * retain
        keys = [k * retain for k in keys]
        key_mix.append([jnp.sum(key * k, axis=1, keepdims=True) for k in keys])
        keys.append(key)
        read_mix.append([jnp.sum(query * k, axis=1, keepdims=True) for k in keys])
        from_state += [reach * key, reach * query]
        values.append(active[2])
        strengths.append(strength)

    spread = one_hot(
        iota((dk, sz.width), 0) == cut * sz.cols + mod(iota((dk, sz.width), 1), sz.cols)
    )
    value_cols = dot(jnp.concatenate(values, axis=0).astype(BF16), spread)
    for copy in copies:
        copy.wait()
    gate_factor(sz, live, gain, gate, factor)
    lane_row = quotient(iota((sz.tile, sz.width), 1), sz.cols)
    own = iota((sz.tile, sz.width), 0) == lane_row
    readouts = [[] for _ in range(T)]
    for at in range(0, n, sz.tile):
        r, g = at // count, at % count
        rows = slice(at, at + sz.tile)
        if sz.whole_tiles:
            block = [
                came[g + i, r * sz.cols : (r + 1) * sz.cols, :] for i in range(sz.tile)
            ]
        else:
            block = [
                came[g + i, : sz.state_rows, :].astype(F32)[r * sz.cols : (r + 1) * sz.cols]
                for i in range(sz.tile)
            ]
        seen = dot(
            jnp.concatenate([x[rows] for x in from_state], axis=0).astype(BF16),
            jnp.concatenate(block, axis=0).astype(BF16),
            1,
            1,
        )
        seen = [seen[i * sz.tile : (i + 1) * sz.tile] for i in range(2 * T)]
        writes = []
        for t in range(T):
            target = value_cols[t * n + at : t * n + at + sz.tile] - seen[2 * t]
            target = jnp.where(own, target, 0.0)
            for s in range(t):
                target = target - key_mix[t][s][rows] * writes[s]
            writes.append(strengths[t][rows] * target)
            read = jnp.where(own, seen[2 * t + 1], 0.0)
            for s in range(t + 1):
                read = read + read_mix[t][s][rows] * writes[s]
            readouts[t].append(read * dk ** (-0.5))
        added = dot(
            jnp.concatenate(writes, axis=0).astype(BF16),
            jnp.concatenate([k[rows] for k in keys], axis=0).astype(BF16),
            0,
            0,
        )
        for i in range(sz.tile):
            part = block[i].astype(F32) * reach[at + i : at + i + 1]
            part = part + added[i * sz.cols : (i + 1) * sz.cols]
            to = scalars[0, at + i]
            if sz.whole_tiles:
                start = pl.multiple_of(mod(to, sz.rows) * sz.cols, sz.cols)
                sent[quotient(to, sz.rows), pl.ds(start, sz.cols), :] = part.astype(BF16)
            else:
                later[pl.ds(pl.multiple_of(to * sz.cols, sz.cols), sz.cols), :] = part
    blocks = [in_block(sz, (n, dk), cut, shift) for shift in range(4)]
    lanes = cut * sz.cols + mod(iota((sz.width, dk), 0), sz.cols)
    fold = [
        one_hot(iota((sz.width, dk), 1) == mod(lanes + shift * sz.quarter, dk))
        for shift in range(-(-T // sz.back_depth))
    ]
    placed = [None] * sz.back_depth
    kept = [None] * sz.back_depth
    for index in range(sz.back_sets):
        shift, slot = index // sz.back_depth, index % sz.back_depth
        if index < T:
            folded = dot(jnp.concatenate(readouts[index], axis=0).astype(BF16), fold[shift])
            value = dot(place[index], folded.astype(BF16))
            placed[slot] = value if placed[slot] is None else placed[slot] + value
        else:
            value = window[(index - T) // sz.parts][(index - T) % sz.parts]
            if shift:
                value = pltpu.roll(value, shift * sz.quarter, 1)
            rest = jnp.zeros((n, dk), F32) if kept[slot] is None else kept[slot]
            kept[slot] = jnp.where(blocks[shift], value, rest)
    held = dot(place[T - 1], jnp.concatenate(kept, axis=1).astype(BF16))
    for slot in range(sz.back_depth):
        value = placed[slot] + held[:, slot * dk : (slot + 1) * dk]
        for r in range(sz.rows):
            at = slot * sz.rows + r
            back[pl.ds(at, count, stride=sz.back_rows), :] = value[r * count : (r + 1) * count]
    for g in range(count):
        p = sz.place_of[g]
        if not sz.whole_tiles:
            sent[p, : sz.state_rows, :] = later[
                p * sz.state_rows : (p + 1) * sz.state_rows, :
            ].astype(BF16)
        sent[p, sz.state_rows :, :] = back[
            g * sz.back_rows : (g + 1) * sz.back_rows, :
        ].astype(BF16)


def unpacker(sz, came, h, wanted):
    shape = (sz.back_rows, sz.dk)
    pieces = [
        came[sz.place_of[h * sz.cuts + cut], sz.state_rows :, :].astype(F32)
        for cut in range(sz.cuts)
    ]
    narrow = {}
    for shift in sorted({index // sz.back_depth for index in wanted}):
        value = pieces[0]
        for cut in range(1, sz.cuts):
            value = jnp.where(in_block(sz, shape, cut, shift), pieces[cut], value)
        if shift:
            value = pltpu.roll(value, sz.dk - shift * sz.quarter, 1)
        narrow[shift] = value

    def unpacked(index):
        at = index % sz.back_depth * sz.rows
        return narrow[index // sz.back_depth][at : at + sz.rows]

    return unpacked


def project_kernel(sz, blocks, factor, weight, came, *refs):
    dk = sz.dk
    partials, kept = refs[: blocks - 1], refs[blocks - 1]
    entries = sz.steps * sz.rows
    padded = factor.shape[0]
    gated = []
    for h in range(sz.heads):
        lanes = slice(h * dk, (h + 1) * dk)
        unpacked = unpacker(sz, came, h, range(sz.steps))
        total = jnp.concatenate(
            [unpacked(t) for t in range(sz.steps)]
            + [jnp.zeros((padded - entries, dk), F32)],
            axis=0,
        )
        scaling = lax.rsqrt(jnp.mean(total * total, axis=1, keepdims=True) + EPSILON)
        gated.append(total * scaling * factor[:, lanes])
    gated = jnp.concatenate(gated, axis=1).astype(BF16)
    kept[...] = gated
    for shift in range(1, blocks):
        project(sz, blocks, shift, gated, weight, partials[shift - 1])


def project(sz, blocks, shift, gated, weight, partial):
    columns = weight.shape[1] // blocks
    lanes = slice(None)
    if blocks > 1:
        at = lax.rem(lax.axis_index("head") + shift, blocks) * columns
        lanes = pl.ds(pl.multiple_of(at, LANES), columns)
    result = dot(gated, weight[:, lanes])
    for t in range(sz.steps):
        partial[t] = result[t * sz.rows : (t + 1) * sz.rows].astype(partial.dtype)


def restore_kernel(sz, blocks, gated, weight, came, states, partial, hist):
    project(sz, blocks, 0, gated[...], weight, partial)
    for h in range(sz.heads):
        unpacked = unpacker(sz, came, h, range(sz.steps, sz.back_sets))
        for tap in range(sz.taps):
            for part in range(sz.parts):
                value = unpacked(sz.steps + tap * sz.parts + part)
                hist[tap, part, :, h * sz.dk : (h + 1) * sz.dk] = value.astype(BF16)
    kind = BF16 if sz.whole_tiles else F32
    for r in range(sz.rows):
        for h in range(sz.heads):
            cuts = [
                came[sz.place_of[h * sz.cuts + cut], : sz.state_rows, :].astype(kind)[
                    r * sz.cols : (r + 1) * sz.cols
                ]
                for cut in range(sz.cuts)
            ]
            states[r, h] = jnp.concatenate(cuts, axis=0).T.astype(F32)


def vmem():
    return pl.BlockSpec(memory_space=pltpu.VMEM)


def smem():
    return pl.BlockSpec(memory_space=pltpu.SMEM)


def anywhere():
    return pl.BlockSpec(memory_space=pl.ANY)


def in_hbm(value):
    return pltpu.with_memory_space_constraint(value, pltpu.HBM)


def call(body, outs, ins, out_specs, scratch, name):
    return pl.pallas_call(
        body,
        out_shape=outs,
        in_specs=ins,
        out_specs=out_specs,
        scratch_shapes=scratch,
        compiler_params=pltpu.CompilerParams(vmem_limit_bytes=VMEM_LIMIT),
        name=name,
    )


def exchange(pieces, groups=None):
    return lax.all_to_all(
        pieces, "rep", split_axis=0, concat_axis=0, axis_index_groups=groups, tiled=True
    )


def local(
    group_total,
    head_total,
    states,
    conv_states,
    projected,
    conv_weight,
    decay_input,
    decay_rate,
    beta_logit,
    out_gate,
    norm_gain,
    out_weight,
    destinations,
    live_counts,
):
    sz = Sizes(group_total, states, conv_states, projected)
    n, channels = sz.groups, sz.heads * sz.dk
    shape = jax.ShapeDtypeStruct
    lives = live_counts.T
    arguments = (
        destinations,
        lives,
        decay_rate.reshape(1, sz.heads),
        beta_logit.transpose(1, 2, 0),
        projected.transpose(0, 2, 1, 3),
        conv_states.transpose(1, 2, 0, 3),
        decay_input,
        conv_weight.transpose(1, 0, 2),
        states,
    )
    routes = shape((sz.steps, sz.slots, sz.slots), BF16)
    pieces, pick, place, final, taps = call(
        functools.partial(pack_kernel, sz),
        (
            shape((n, sz.state_rows + sz.info_rows, sz.dk), BF16),
            routes,
            routes,
            shape((8, sz.slots), jnp.int32),
            shape((sz.parts, sz.taps + 1, sz.dk), F32),
        ),
        [anywhere()] * len(arguments),
        (vmem(),) * 5,
        [pltpu.VMEM(x.shape, x.dtype) for x in arguments]
        + [
            pltpu.VMEM((sz.heads, sz.value_at, sz.dk), F32),
            pltpu.VMEM((4, sz.heads, sz.tail_rows, sz.dk), F32),
            pltpu.VMEM((sz.heads, sz.dk), F32),
            pltpu.SemaphoreType.DMA((len(arguments) - 1 + sz.rows * sz.heads,)),
        ],
        "pack",
    )(*[in_hbm(x) for x in arguments])
    came = exchange(pieces)
    padded = round_up(sz.steps * sz.rows, 16)
    gain = norm_gain.reshape(1, sz.dk)
    stepped, factor = call(
        functools.partial(step_kernel, sz),
        (
            shape((n, sz.state_rows + sz.back_rows, sz.dk), BF16),
            shape((padded, channels), F32),
        ),
        [vmem()] * 4 + [anywhere()] * 4,
        (vmem(), vmem()),
        [
            pltpu.SMEM((8, sz.slots), jnp.int32),
            pltpu.VMEM(lives.shape, lives.dtype),
            pltpu.VMEM(gain.shape, F32),
            pltpu.VMEM(out_gate.shape, BF16),
            pltpu.VMEM((n * sz.info_rows, sz.dk), F32),
            pltpu.VMEM((8 if sz.whole_tiles else n * sz.state_rows, sz.dk), F32),
            pltpu.VMEM((n * sz.back_rows, sz.dk), F32),
            pltpu.SemaphoreType.DMA((4,)),
        ],
        "steps",
    )(taps, pick, place, came, final, in_hbm(lives), in_hbm(gain), in_hbm(out_gate))
    back = exchange(stepped, [sz.order])
    width = out_weight.shape[1]
    columns = width // head_total
    blocks = head_total if columns % LANES == 0 else 1
    *partials, gated = call(
        functools.partial(project_kernel, sz, blocks),
        tuple(shape((sz.steps, sz.rows, columns), BF16) for _ in range(1, blocks))
        + (shape((padded, channels), BF16),),
        [vmem()] * 3,
        tuple([vmem()] * blocks),
        [],
        "project",
    )(factor, out_weight, back)
    states_out, own, conv_out = call(
        functools.partial(restore_kernel, sz, blocks),
        (
            shape(states.shape, F32),
            shape((sz.steps, sz.rows, width // blocks), F32),
            shape((sz.taps, sz.parts, sz.rows, channels), BF16),
        ),
        [vmem()] * 3,
        (vmem(),) * 3,
        [],
        "restore",
    )(gated, out_weight, back)
    partials = [own, *partials]
    if blocks != head_total:
        mine = lax.axis_index("head")
        partials = [
            lax.dynamic_slice_in_dim(
                partials[0], lax.rem(mine + shift, head_total) * columns, columns, 2
            )
            for shift in range(head_total)
        ]
    total = partials[0]
    for shift in range(1, head_total):
        pairs = [(i, (i + shift) % head_total) for i in range(head_total)]
        passed = lax.ppermute(partials[shift].astype(BF16), "head", pairs)
        total = total + passed.astype(F32)
    return (total.astype(BF16), states_out, conv_out.transpose(2, 0, 1, 3))


def solution(mesh):
    placed = (
        P("rep", "head", None, None),
        P("rep", None, None, "head"),
        P(None, "rep", None, "head"),
        P(None, None, "head"),
        P(None, "rep", "head"),
        P("head"),
        P(None, "rep", "head"),
        P(None, "rep", "head"),
        P(),
        P("head", None),
        P(),
        P(None, "rep"),
    )
    return jax.shard_map(
        functools.partial(local, mesh.shape["rep"], mesh.shape["head"]),
        mesh=mesh,
        in_specs=placed,
        out_specs=(
            P(None, "rep", "head"),
            P("rep", "head", None, None),
            P("rep", None, None, "head"),
        ),
        check_vma=False,
    )
```

profile of v0, /device:TPU:0, one launch (start us, length us, event | category | flops | bytes accessed | tf_op | source)
XLA Modules:
  0.0 44.7 jit_solution(8643585870801538270)
XLA Ops:
  0.6 0.0 copy-start
  0.6 2.1 %pack.1 = (bf16[16,120,128]{2,1,0:T(8,128)(2,1)S(1)}, bf16[6,32,32]{2,1,0:T(8,128)(2,1)S(1)}, bf16[6,32,32]{2,1,0:T(8,128)(2,1)S(1)}, s32[8,32]{1,0:T(8,128)S(1)}, f32[3,4,128]{2,1,0:T(4,128)S(1)}) custom-call(s32[6,32]{1,0:T(8,128)} %refs_0_.1, s32[1,6]{1,0:T(1,128)} %bitcast.12, f32[1,4]{1,0:T(1,128)} %bitcast.14, f32[2,4,6]{2,1,0:T(4,128)} %bitcast.11, ...), custom_call_target="tpu_custom_call" | custom-call | tf_op jit(solution)/shard_map/pack/pallas_call | solution.py:512
  2.7 20.9 %all_to_all.10.came = bf16[16,120,128]{2,1,0:T(8,128)(2,1)S(1)} all-to-all(bf16[16,120,128]{2,1,0:T(8,128)(2,1)S(1)} %get-tuple-element.18), channel_id=1, replica_groups=mesh['rep'=16,'head'=2] {'rep'}, dimensions={0} | all-to-all | bytes 983040 | tf_op jit(solution)/shard_map/all_to_all | solution.py:475
  23.7 1.8 %steps.1 = (bf16[16,72,128]{2,1,0:T(8,128)(2,1)S(1)}, f32[16,512]{1,0:T(8,128)S(1)}) custom-call(f32[3,4,128]{2,1,0:T(4,128)S(1)} %get-tuple-element.15.filters, bf16[6,32,32]{2,1,0:T(8,128)(2,1)S(1)} %get-tuple-element.16.pick, bf16[6,32,32]{2,1,0:T(8,128)(2,1)S(1)} %get-tuple-element.17.place, bf16[16,120,128]{2,1,0:T(8,128)(2,1)S(1)} %all_to_all.10.came, ...), custom_call_target="tpu_custom_call" | custom-call | tf_op jit(solution)/shard_map/steps/pallas_call | solution.py:535
  25.5 14.2 %all_to_all.11.came = bf16[16,72,128]{2,1,0:T(8,128)(2,1)S(1)} all-to-all(bf16[16,72,128]{2,1,0:T(8,128)(2,1)S(1)} %get-tuple-element.21), channel_id=1, replica_groups={{0,16,8,24,2,18,10,26,4,20,12,28,6,22,14,30},{1,17,9,25,3,19,11,27,5,21..., dimensions={0} | all-to-all | bytes 589824 | tf_op jit(solution)/shard_map/all_to_all | solution.py:475
  39.7 0.0 copy-done
  39.7 0.4 project.1
  40.1 1.6 %collective-permute-start = (bf16[6,2,1152]{2,1,0:T(2,128)(2,1)S(1)}, bf16[6,2,1152]{2,1,0:T(2,128)(2,1)S(1)}, u32[]{:S(2)}, u32[]{:S(2)}) collective-permute-start(bf16[6,2,1152]{2,1,0:T(2,128)(2,1)S(1)} %get-tuple-element.24), channel_id=1, source_target_pairs={{0,1},{1,0},{2,3},{3,2},{4,5},{5,4},{6,7},{7,6},{8,9},{9,8},{10,11... | collective-permute-start | bytes 82952 | tf_op jit(solution)/shard_map/ppermute | solution.py:592
  41.7 1.0 %restore.1 = (f32[2,4,128,128]{3,2,1,0:T(8,128)}, f32[6,2,1152]{2,1,0:T(2,128)S(1)}, bf16[3,3,2,512]{3,2,1,0:T(2,128)(2,1)}) custom-call(bf16[16,512]{1,0:T(8,128)(2,1)S(1)} %get-tuple-element.22.gated, bf16[512,2304]{1,0:T(8,128)(2,1)S(1)} %copy-done, bf16[16,72,128]{2,1,0:T(8,128)(2,1)S(1)} %all_to_all.11.came), custom_call_target="tpu_custom_call" | custom-call | tf_op jit(solution)/shard_map/restore/pallas_call | solution.py:568
  42.7 1.3 %collective-permute-done = bf16[6,2,1152]{2,1,0:T(2,128)(2,1)S(1)} collective-permute-done((bf16[6,2,1152]{2,1,0:T(2,128)(2,1)S(1)}, bf16[6,2,1152]{2,1,0:T(2,128)(2,1)S(1)}, u32[]{:S(2)}, u32[]{:S(2)}) %collective-permute-start) | collective-permute-done | bytes 27680 | tf_op jit(solution)/shard_map/ppermute | solution.py:592
  44.0 0.6 %add_convert_fusion = bf16[6,2,1152]{2,1,0:T(2,128)(2,1)} fusion(f32[6,2,1152]{2,1,0:T(2,128)S(1)} %get-tuple-element.23, bf16[6,2,1152]{2,1,0:T(2,128)(2,1)S(1)} %collective-permute-done), kind=kLoop, calls=%fused_computation | loop fusion | flops 41472 | bytes 110592 | tf_op jit(solution)/shard_map/convert_element_type | solution.py:594
Async XLA Ops:
  0.6 39.1 %copy-start = (bf16[512,2304]{1,0:T(8,128)(2,1)S(1)}, bf16[512,2304]{1,0:T(8,128)(2,1)}, u32[]{:S(2)}) copy-start(bf16[512,2304]{1,0:T(8,128)(2,1)} %weight.3) | copy-start | bytes 7077892
  40.1 3.9 %collective-permute-start = (bf16[6,2,1152]{2,1,0:T(2,128)(2,1)S(1)}, bf16[6,2,1152]{2,1,0:T(2,128)(2,1)S(1)}, u32[]{:S(2)}, u32[]{:S(2)}) collective-permute-start(bf16[6,2,1152]{2,1,0:T(2,128)(2,1)S(1)} %get-tuple-element.24), channel_id=1, source_target_pairs={{0,1},{1,0},{2,3},{3,2},{4,5},{5,4},{6,7},{7,6},{8,9},{9,8},{10,11... | collective-permute-start | bytes 82952 | tf_op jit(solution)/shard_map/ppermute | solution.py:592
where the time goes:
time: 45 us; the launch traced here: 44.7 us
  blocking collectives  35.2 us (78%)
  Pallas kernels  5.32 us (12%)
  starting transfers between devices  1.58 us (4%)
  waiting for transfers between devices  1.31 us (3%)
  between operations  0.66 us (1%)
  other arithmetic  0.64 us (1%)
    all_to_all x2, blocking collectives, exchange(): lax.all_to_all(pieces, 'rep', split_axis=0, concat_axis=0, axis_index_gro...  35.2 us
    pallas_call x1, Pallas kernels, local(): call(functools.partial(pack_kernel, sz), (shape((n, sz.state_rows + sz.in...  2.1 us
    pallas_call x1, Pallas kernels, local(): call(functools.partial(step_kernel, sz), (shape((n, sz.state_rows + sz.ba...  1.79 us
    ppermute x1, starting transfers between devices, local(): passed = lax.ppermute(partials[shift].astype(BF16), 'head', pairs)  1.58 us
    ppermute x1, waiting for transfers between devices, local(): passed = lax.ppermute(partials[shift].astype(BF16), 'head', pairs)  1.31 us
    pallas_call x1, Pallas kernels, local(): call(functools.partial(restore_kernel, sz, blocks), (shape(states.shape,...  1.04 us
  transfers between devices with their start and end apart: 1, of which 1 were waited for; matrix products, arithmetic and copies ran while one was open for 0% of the time, Pallas kernels for 2%

commit v1 on v0

--- a/solution.py
+++ b/solution.py
@@ -32,19 +32,28 @@
         self.cols = self.dk // self.cuts
         self.state_rows = self.rows * self.cols
         self.quarter = self.dk // 4
-        self.decay_at = self.steps * 2 * self.rows
-        self.hist_at = self.decay_at + self.steps * self.rows
-        self.value_at = self.hist_at + self.taps * 2 * self.rows
+        self.decay_at = self.steps * 2
+        self.hist_at = self.decay_at + self.steps
+        self.value_at = self.hist_at + self.taps * 2
         self.value_depth = -(-(self.steps + self.taps) // 4)
-        self.flag_at = self.value_depth * self.rows
-        self.tail_rows = round_up(self.flag_at + self.rows, 8)
-        self.info_rows = self.value_at + self.tail_rows
+        self.flag_at = self.value_at + self.value_depth
+        self.info_sets = self.padded(self.flag_at + 1)
+        self.info_rows = self.rows * self.info_sets
         self.back_sets = self.steps + self.taps * self.parts
-        self.back_depth = -(-self.back_sets // 4)
-        self.back_rows = round_up(self.back_depth * self.rows, 8)
+        self.back_depth = self.padded(-(-self.back_sets // 4))
+        self.back_rows = self.rows * self.back_depth
+        self.read_rows = round_up(-(-self.steps // self.back_depth) * self.back_rows, 16)
         self.whole_tiles = self.cols % 16 == 0
         self.width = max(LANES, 8 * self.cols)
         self.tile = self.width // self.cols
+
+    def padded(self, sets):
+        while sets * self.rows % 8:
+            sets += 1
+        return sets
+
+    def read_at(self, t, r):
+        return t // self.back_depth * self.back_rows + r * self.back_depth + t % self.back_depth
 
 
 def mod(value, size):
@@ -108,35 +117,35 @@
         rates = jnp.where(lane_head == h, rate[:, h : h + 1], rates)
     row_ids = iota((sz.rows, channels), 0)
 
-    def keep(target, at, value):
+    def keep(target, index, value):
         for h in range(sz.heads):
-            target[h, at : at + sz.rows, :] = value[:, h * dk : (h + 1) * dk]
-
-    tails[...] = jnp.zeros(tails.shape, F32)
+            rows = pl.ds(index, sz.rows, stride=sz.info_sets)
+            target[h, rows, :] = value[:, h * dk : (h + 1) * dk]
 
     def keep_value(index, value):
         shift = index // sz.value_depth
-        at = index % sz.value_depth * sz.rows
-        for h in range(sz.heads):
-            own = value[:, h * dk : (h + 1) * dk]
-            if shift:
-                own = pltpu.roll(own, shift * sz.quarter, 1)
-            tails[shift, h, at : at + sz.rows, :] = own
+        at = sz.value_at + index % sz.value_depth
+        if shift:
+            heads = [value[:, h * dk : (h + 1) * dk] for h in range(sz.heads)]
+            heads = [pltpu.roll(head, shift * sz.quarter, 1) for head in heads]
+            keep(tails.at[shift - 1], at, jnp.concatenate(heads, axis=1))
+        else:
+            keep(info, at, value)
 
     for t in range(sz.steps):
         for part in range(2):
-            keep(info, (t * 2 + part) * sz.rows, proj[t, part].astype(F32))
+            keep(info, t * 2 + part, proj[t, part].astype(F32))
         keep_value(t, proj[t, 2].astype(F32))
         x = decay[t]
         softplus = jnp.maximum(x, 0.0) + jnp.log1p(jnp.exp(-jnp.abs(x)))
         keep(
             info,
-            sz.decay_at + t * sz.rows,
+            sz.decay_at + t,
             jnp.where(row_ids < live[:, t : t + 1], rates * softplus, 0.0),
         )
     for tap in range(sz.taps):
         for part in range(2):
-            keep(info, sz.hist_at + (tap * 2 + part) * sz.rows, hist[tap, part].astype(F32))
+            keep(info, sz.hist_at + tap * 2 + part, hist[tap, part].astype(F32))
         keep_value(sz.steps + tap, hist[tap, 2].astype(F32))
     lane = iota((sz.heads, dk), 1)
     strengths[...] = jnp.zeros(strengths.shape, F32)
@@ -149,37 +158,42 @@
         high = strength.astype(BF16).astype(F32)
         flags = high + pltpu.roll(lives, 16, 1) + pltpu.roll(strength - high, 32, 1)
         for h in range(sz.heads):
-            at = sz.flag_at + r
-            for shift in range(4):
-                tails[shift, h, at : at + 1, :] = flags[h : h + 1]
-    blocks = [
-        [in_block(sz, (sz.tail_rows, dk), cut, shift) for shift in range(1, 4)]
-        for cut in range(sz.cuts)
+            at = r * sz.info_sets + sz.flag_at
+            info[h, at : at + 1, :] = flags[h : h + 1]
+    wide = [
+        r * sz.info_sets + sz.value_at + i for r in range(sz.rows) for i in range(sz.value_depth)
     ]
+    masks = {}
+    for tile in sorted({at // 8 for at in wide}):
+        row = iota((8, dk), 0) + tile * 8
+        narrow = functools.reduce(jnp.logical_or, [row == at for at in wide if at // 8 == tile])
+        masks[tile] = [
+            [narrow & in_block(sz, (8, dk), cut, shift) for shift in range(1, 4)]
+            for cut in range(sz.cuts)
+        ]
     for h in range(sz.heads):
-        head = info[h].astype(BF16)
         across = [states[r, h].T for r in range(sz.rows)]
+        base = [info[h, at : at + 8, :] for at in range(0, sz.info_rows, 8)]
+        others = {
+            tile: [tails[shift, h, tile * 8 : tile * 8 + 8, :] for shift in range(3)]
+            for tile in masks
+        }
         for cut in range(sz.cuts):
             p, at = h * sz.cuts + cut, cut * sz.cols
             own = [a[at : at + sz.cols] for a in across]
             pieces[p, : sz.state_rows, :] = jnp.concatenate(own, axis=0).astype(BF16)
-            pieces[p, sz.state_rows : sz.state_rows + sz.value_at, :] = head
-            tail = tails[0, h]
-            for shift in range(1, 4):
-                tail = jnp.where(blocks[cut][shift - 1], tails[shift, h], tail)
-            pieces[p, sz.state_rows + sz.value_at :, :] = tail.astype(BF16)
+            rest = list(base)
+            for tile in masks:
+                for shift in range(3):
+                    rest[tile] = jnp.where(
+                        masks[tile][cut][shift], others[tile][shift], rest[tile]
+                    )
+            pieces[p, sz.state_rows :, :] = jnp.concatenate(rest, axis=0).astype(BF16)
 
 
 def route(sz, targets, pick, place, final):
     n, T = sz.slots, sz.steps
-
-    def label(slot):
-        return mod(slot, sz.rows) * sz.groups + quotient(slot, sz.rows)
-
-    to_label = one_hot(label(iota((n, n), 0)) == iota((n, n), 1))
-    ordered = dot(targets[...].astype(F32).astype(BF16), to_label)
-    ordered = label((ordered + 0.5).astype(jnp.int32))
-    steps = [one_hot(iota((n, n), 0) == ordered[t : t + 1]) for t in range(T)]
+    steps = [one_hot(iota((n, n), 0) == targets[t : t + 1, :]) for t in range(T)]
     chain = [steps[0]]
     for t in range(1, T):
         if t % 2:
@@ -191,7 +205,7 @@
         place[t] = chain[t]
         pick[t] = chain[t].astype(F32).T.astype(BF16)
     slot = iota((8, n), 1)
-    row, group = quotient(slot, sz.groups), mod(slot, sz.groups)
+    row, group = mod(slot, sz.rows), quotient(slot, sz.rows)
     head, cut = quotient(group, sz.cuts), mod(group, sz.cuts)
     far = quotient(head, 2) + mod(head, 2) * ((sz.heads + 1) // 2)
     weights = (cut * sz.heads + far) * sz.rows + row
@@ -206,9 +220,10 @@
     factor[...] = jnp.zeros(factor.shape, F32)
     for t in range(sz.steps):
         gates = gains / (1.0 + jnp.exp(-gate[t].astype(F32)))
-        factor[t * sz.rows : (t + 1) * sz.rows, :] = jnp.where(
-            row < live[:, t : t + 1], gates, 0.0
-        )
+        gates = jnp.where(row < live[:, t : t + 1], gates, 0.0)
+        for r in range(sz.rows):
+            at = sz.read_at(t, r)
+            factor[at : at + 1, :] = gates[r : r + 1]
 
 
 def step_kernel(sz, filters, pick, place, came, *refs):
@@ -226,20 +241,18 @@
     for g in range(count):
         info[g * stride : (g + 1) * stride, :] = came[g, sz.state_rows :, :].astype(F32)
 
-    def gather(at):
-        return jnp.concatenate(
-            [info[pl.ds(at + r, count, stride=stride), :] for r in range(sz.rows)], axis=0
-        )
+    def gather(index):
+        return info[pl.ds(index, n, stride=sz.info_sets), :]
 
     def gather_value(index):
-        value = gather(sz.value_at + index % sz.value_depth * sz.rows)
+        value = gather(sz.value_at + index % sz.value_depth)
         shift = index // sz.value_depth
-        return pltpu.roll(value, sz.dk - shift * sz.quarter, 1) if shift else value
+        return pltpu.roll(value, dk - shift * sz.quarter, 1) if shift else value
 
     weights = [filters[part] for part in range(sz.parts)]
-    flags = gather(sz.value_at + sz.flag_at)
+    flags = gather(sz.flag_at)
     window = [
-        [gather(sz.hist_at + (tap * 2 + part) * sz.rows) for part in range(2)]
+        [gather(sz.hist_at + tap * 2 + part) for part in range(2)]
         + [gather_value(T + tap)]
         for tap in range(sz.taps)
     ]
@@ -247,8 +260,8 @@
     keys = []
     from_state, values, strengths, key_mix, read_mix = [], [], [], [], []
     for t in range(T):
-        slots = [gather((t * 2 + part) * sz.rows) for part in range(2)]
-        slots += [gather_value(t), gather(sz.decay_at + t * sz.rows), flags]
+        slots = [gather(t * 2 + part) for part in range(2)]
+        slots += [gather_value(t), gather(sz.decay_at + t), flags]
         moved = dot(pick[t], jnp.concatenate(slots, axis=1).astype(BF16))
         inputs = [moved[:, i * dk : (i + 1) * dk] for i in range(sz.parts + 2)]
         moved_flags = inputs[sz.parts + 1]
@@ -287,17 +300,15 @@
     own = iota((sz.tile, sz.width), 0) == lane_row
     readouts = [[] for _ in range(T)]
     for at in range(0, n, sz.tile):
-        r, g = at // count, at % count
         rows = slice(at, at + sz.tile)
-        if sz.whole_tiles:
-            block = [
-                came[g + i, r * sz.cols : (r + 1) * sz.cols, :] for i in range(sz.tile)
-            ]
-        else:
-            block = [
-                came[g + i, : sz.state_rows, :].astype(F32)[r * sz.cols : (r + 1) * sz.cols]
-                for i in range(sz.tile)
-            ]
+        block = []
+        for g in range(at // sz.rows, (at + sz.tile) // sz.rows):
+            for r in range(sz.rows):
+                if sz.whole_tiles:
+                    block.append(came[g, r * sz.cols : (r + 1) * sz.cols, :])
+                else:
+                    piece = came[g, : sz.state_rows, :].astype(F32)
+                    block.append(piece[r * sz.cols : (r + 1) * sz.cols])
         seen = dot(
             jnp.concatenate([x[rows] for x in from_state], axis=0).astype(BF16),
             jnp.concatenate(block, axis=0).astype(BF16),
@@ -351,12 +362,13 @@
                 value = pltpu.roll(value, shift * sz.quarter, 1)
             rest = jnp.zeros((n, dk), F32) if kept[slot] is None else kept[slot]
             kept[slot] = jnp.where(blocks[shift], value, rest)
+    kept = [jnp.zeros((n, dk), F32) if value is None else value for value in kept]
     held = dot(place[T - 1], jnp.concatenate(kept, axis=1).astype(BF16))
     for slot in range(sz.back_depth):
-        value = placed[slot] + held[:, slot * dk : (slot + 1) * dk]
-        for r in range(sz.rows):
-            at = slot * sz.rows + r
-            back[pl.ds(at, count, stride=sz.back_rows), :] = value[r * count : (r + 1) * count]
+        value = held[:, slot * dk : (slot + 1) * dk]
+        if placed[slot] is not None:
+            value = value + placed[slot]
+        back[pl.ds(slot, n, stride=sz.back_depth), :] = value
     for g in range(count):
         p = sz.place_of[g]
         if not sz.whole_tiles:
@@ -368,7 +380,7 @@
         ].astype(BF16)
 
 
-def unpacker(sz, came, h, wanted):
+def unpack(sz, came, h, wanted):
     shape = (sz.back_rows, sz.dk)
     pieces = [
         came[sz.place_of[h * sz.cuts + cut], sz.state_rows :, :].astype(F32)
@@ -383,27 +395,21 @@
             value = pltpu.roll(value, sz.dk - shift * sz.quarter, 1)
         narrow[shift] = value
 
-    def unpacked(index):
-        at = index % sz.back_depth * sz.rows
-        return narrow[index // sz.back_depth][at : at + sz.rows]
-
-    return unpacked
+    return narrow
 
 
 def project_kernel(sz, blocks, factor, weight, came, *refs):
     dk = sz.dk
     partials, kept = refs[: blocks - 1], refs[blocks - 1]
-    entries = sz.steps * sz.rows
-    padded = factor.shape[0]
     gated = []
     for h in range(sz.heads):
         lanes = slice(h * dk, (h + 1) * dk)
-        unpacked = unpacker(sz, came, h, range(sz.steps))
-        total = jnp.concatenate(
-            [unpacked(t) for t in range(sz.steps)]
-            + [jnp.zeros((padded - entries, dk), F32)],
-            axis=0,
-        )
+        narrow = unpack(sz, came, h, range(sz.steps))
+        total = [narrow[quarter] for quarter in sorted(narrow)]
+        spare = sz.read_rows - len(total) * sz.back_rows
+        if spare:
+            total.append(jnp.zeros((spare, dk), F32))
+        total = jnp.concatenate(total, axis=0)
         scaling = lax.rsqrt(jnp.mean(total * total, axis=1, keepdims=True) + EPSILON)
         gated.append(total * scaling * factor[:, lanes])
     gated = jnp.concatenate(gated, axis=1).astype(BF16)
@@ -420,16 +426,21 @@
         lanes = pl.ds(pl.multiple_of(at, LANES), columns)
     result = dot(gated, weight[:, lanes])
     for t in range(sz.steps):
-        partial[t] = result[t * sz.rows : (t + 1) * sz.rows].astype(partial.dtype)
+        rows = [result[at : at + 1] for at in (sz.read_at(t, r) for r in range(sz.rows))]
+        partial[t] = jnp.concatenate(rows, axis=0).astype(partial.dtype)
 
 
 def restore_kernel(sz, blocks, gated, weight, came, states, partial, hist):
     project(sz, blocks, 0, gated[...], weight, partial)
     for h in range(sz.heads):
-        unpacked = unpacker(sz, came, h, range(sz.steps, sz.back_sets))
+        narrow = unpack(sz, came, h, range(sz.steps, sz.back_sets))
         for tap in range(sz.taps):
             for part in range(sz.parts):
-                value = unpacked(sz.steps + tap * sz.parts + part)
+                index = sz.steps + tap * sz.parts + part
+                held = narrow[index // sz.back_depth]
+                at = index % sz.back_depth
+                rows = [held[at + r * sz.back_depth :][:1] for r in range(sz.rows)]
+                value = jnp.concatenate(rows, axis=0)
                 hist[tap, part, :, h * sz.dk : (h + 1) * sz.dk] = value.astype(BF16)
     kind = BF16 if sz.whole_tiles else F32
     for r in range(sz.rows):
@@ -522,21 +533,20 @@
         (vmem(),) * 5,
         [pltpu.VMEM(x.shape, x.dtype) for x in arguments]
         + [
-            pltpu.VMEM((sz.heads, sz.value_at, sz.dk), F32),
-            pltpu.VMEM((4, sz.heads, sz.tail_rows, sz.dk), F32),
+            pltpu.VMEM((sz.heads, sz.info_rows, sz.dk), F32),
+            pltpu.VMEM((3, sz.heads, sz.info_rows, sz.dk), F32),
             pltpu.VMEM((sz.heads, sz.dk), F32),
             pltpu.SemaphoreType.DMA((len(arguments) - 1 + sz.rows * sz.heads,)),
         ],
         "pack",
     )(*[in_hbm(x) for x in arguments])
     came = exchange(pieces)
-    padded = round_up(sz.steps * sz.rows, 16)
     gain = norm_gain.reshape(1, sz.dk)
     stepped, factor = call(
         functools.partial(step_kernel, sz),
         (
             shape((n, sz.state_rows + sz.back_rows, sz.dk), BF16),
-            shape((padded, channels), F32),
+            shape((sz.read_rows, channels), F32),
         ),
         [vmem()] * 4 + [anywhere()] * 4,
         (vmem(), vmem()),
@@ -559,7 +569,7 @@
     *partials, gated = call(
         functools.partial(project_kernel, sz, blocks),
         tuple(shape((sz.steps, sz.rows, columns), BF16) for _ in range(1, blocks))
-        + (shape((padded, channels), BF16),),
+        + (shape((sz.read_rows, channels), BF16),),
         [vmem()] * 3,
         tuple([vmem()] * blocks),
         [],

time: 45 us -> 45 us (level)
  no operation moved by 1% of the time
where the time goes in v1:
time: 45 us; the launch traced here: 44.7 us
  blocking collectives  35.2 us (78%)
  Pallas kernels  5.32 us (12%)
  starting transfers between devices  1.58 us (4%)
  waiting for transfers between devices  1.31 us (3%)
  between operations  0.67 us (1%)
  other arithmetic  0.64 us (1%)
    all_to_all x2, blocking collectives, exchange(): lax.all_to_all(pieces, 'rep', split_axis=0, concat_axis=0, axis_index_gro...  35.2 us
    pallas_call x1, Pallas kernels, local(): call(functools.partial(pack_kernel, sz), (shape((n, sz.state_rows + sz.in...  1.97 us
    pallas_call x1, Pallas kernels, local(): call(functools.partial(step_kernel, sz), (shape((n, sz.state_rows + sz.ba...  1.91 us
    ppermute x1, starting transfers between devices, local(): passed = lax.ppermute(partials[shift].astype(BF16), 'head', pairs)  1.58 us
    ppermute x1, waiting for transfers between devices, local(): passed = lax.ppermute(partials[shift].astype(BF16), 'head', pairs)  1.31 us
    pallas_call x1, Pallas kernels, local(): call(functools.partial(restore_kernel, sz, blocks), (shape(states.shape,...  1.03 us
  transfers between devices with their start and end apart: 1, of which 1 were waited for; matrix products, arithmetic and copies ran while one was open for 0% of the time, Pallas kernels for 2%

profile of v1, /device:TPU:0, one launch (start us, length us, event | category | flops | bytes accessed | tf_op | source)
XLA Modules:
  0.0 44.7 jit_solution(13453981585672811478)
XLA Ops:
  0.6 0.0 copy-start
  0.6 2.0 %pack.1 = (bf16[16,120,128]{2,1,0:T(8,128)(2,1)S(1)}, bf16[6,32,32]{2,1,0:T(8,128)(2,1)S(1)}, bf16[6,32,32]{2,1,0:T(8,128)(2,1)S(1)}, s32[8,32]{1,0:T(8,128)S(1)}, f32[3,4,128]{2,1,0:T(4,128)S(1)}) custom-call(s32[6,32]{1,0:T(8,128)} %refs_0_.1, s32[1,6]{1,0:T(1,128)} %bitcast.12, f32[1,4]{1,0:T(1,128)} %bitcast.14, f32[2,4,6]{2,1,0:T(4,128)} %bitcast.11, ...), custom_call_target="tpu_custom_call" | custom-call | tf_op jit(solution)/shard_map/pack/pallas_call | solution.py:523
  2.6 20.9 %all_to_all.10.came = bf16[16,120,128]{2,1,0:T(8,128)(2,1)S(1)} all-to-all(bf16[16,120,128]{2,1,0:T(8,128)(2,1)S(1)} %get-tuple-element.18), channel_id=1, replica_groups=mesh['rep'=16,'head'=2] {'rep'}, dimensions={0} | all-to-all | bytes 983040 | tf_op jit(solution)/shard_map/all_to_all | solution.py:486
  23.6 1.9 %steps.1 = (bf16[16,72,128]{2,1,0:T(8,128)(2,1)S(1)}, f32[16,512]{1,0:T(8,128)S(1)}) custom-call(f32[3,4,128]{2,1,0:T(4,128)S(1)} %get-tuple-element.15.filters, bf16[6,32,32]{2,1,0:T(8,128)(2,1)S(1)} %get-tuple-element.16.pick, bf16[6,32,32]{2,1,0:T(8,128)(2,1)S(1)} %get-tuple-element.17.place, bf16[16,120,128]{2,1,0:T(8,128)(2,1)S(1)} %all_to_all.10.came, ...), custom_call_target="tpu_custom_call" | custom-call | tf_op jit(solution)/shard_map/steps/pallas_call | solution.py:545
  25.5 14.2 %all_to_all.11.came = bf16[16,72,128]{2,1,0:T(8,128)(2,1)S(1)} all-to-all(bf16[16,72,128]{2,1,0:T(8,128)(2,1)S(1)} %get-tuple-element.21), channel_id=1, replica_groups={{0,16,8,24,2,18,10,26,4,20,12,28,6,22,14,30},{1,17,9,25,3,19,11,27,5,21..., dimensions={0} | all-to-all | bytes 589824 | tf_op jit(solution)/shard_map/all_to_all | solution.py:486
  39.7 0.0 copy-done
  39.7 0.4 project.1
  40.1 1.6 %collective-permute-start = (bf16[6,2,1152]{2,1,0:T(2,128)(2,1)S(1)}, bf16[6,2,1152]{2,1,0:T(2,128)(2,1)S(1)}, u32[]{:S(2)}, u32[]{:S(2)}) collective-permute-start(bf16[6,2,1152]{2,1,0:T(2,128)(2,1)S(1)} %get-tuple-element.24), channel_id=1, source_target_pairs={{0,1},{1,0},{2,3},{3,2},{4,5},{5,4},{6,7},{7,6},{8,9},{9,8},{10,11... | collective-permute-start | bytes 82952 | tf_op jit(solution)/shard_map/ppermute | solution.py:602
  41.7 1.0 %restore.1 = (f32[2,4,128,128]{3,2,1,0:T(8,128)}, f32[6,2,1152]{2,1,0:T(2,128)S(1)}, bf16[3,3,2,512]{3,2,1,0:T(2,128)(2,1)}) custom-call(bf16[16,512]{1,0:T(8,128)(2,1)S(1)} %get-tuple-element.22.gated, bf16[512,2304]{1,0:T(8,128)(2,1)S(1)} %copy-done, bf16[16,72,128]{2,1,0:T(8,128)(2,1)S(1)} %all_to_all.11.came), custom_call_target="tpu_custom_call" | custom-call | tf_op jit(solution)/shard_map/restore/pallas_call | solution.py:578
  42.7 1.3 %collective-permute-done = bf16[6,2,1152]{2,1,0:T(2,128)(2,1)S(1)} collective-permute-done((bf16[6,2,1152]{2,1,0:T(2,128)(2,1)S(1)}, bf16[6,2,1152]{2,1,0:T(2,128)(2,1)S(1)}, u32[]{:S(2)}, u32[]{:S(2)}) %collective-permute-start) | collective-permute-done | bytes 27680 | tf_op jit(solution)/shard_map/ppermute | solution.py:602
  44.0 0.6 %add_convert_fusion = bf16[6,2,1152]{2,1,0:T(2,128)(2,1)} fusion(f32[6,2,1152]{2,1,0:T(2,128)S(1)} %get-tuple-element.23, bf16[6,2,1152]{2,1,0:T(2,128)(2,1)S(1)} %collective-permute-done), kind=kLoop, calls=%fused_computation | loop fusion | flops 41472 | bytes 110592 | tf_op jit(solution)/shard_map/convert_element_type | solution.py:604
Async XLA Ops:
  0.6 39.1 %copy-start = (bf16[512,2304]{1,0:T(8,128)(2,1)S(1)}, bf16[512,2304]{1,0:T(8,128)(2,1)}, u32[]{:S(2)}) copy-start(bf16[512,2304]{1,0:T(8,128)(2,1)} %weight.3) | copy-start | bytes 7077892
  40.1 3.9 %collective-permute-start = (bf16[6,2,1152]{2,1,0:T(2,128)(2,1)S(1)}, bf16[6,2,1152]{2,1,0:T(2,128)(2,1)S(1)}, u32[]{:S(2)}, u32[]{:S(2)}) collective-permute-start(bf16[6,2,1152]{2,1,0:T(2,128)(2,1)S(1)} %get-tuple-element.24), channel_id=1, source_target_pairs={{0,1},{1,0},{2,3},{3,2},{4,5},{5,4},{6,7},{7,6},{8,9},{9,8},{10,11... | collective-permute-start | bytes 82952 | tf_op jit(solution)/shard_map/ppermute | solution.py:602

commit v2 on v1

--- a/solution.py
+++ b/solution.py
@@ -103,7 +103,7 @@
     for r in range(sz.rows):
         for h in range(sz.heads):
             start(states_hbm.at[r, h], states.at[r, h])
-    for copy in copies:
+    for copy in copies[:count]:
         copy.wait()
     route(sz, targets, pick, place, final)
     own_head = lax.axis_index("rep") // sz.cuts
@@ -171,24 +171,34 @@
             [narrow & in_block(sz, (8, dk), cut, shift) for shift in range(1, 4)]
             for cut in range(sz.cuts)
         ]
+    shared = [
+        at for at in range(0, sz.info_rows, 16) if at // 8 not in masks and at // 8 + 1 not in masks
+    ]
+    held = [[info[h, at : at + 16, :].astype(BF16) for at in shared] for h in range(sz.heads)]
+    for copy in copies[count:]:
+        copy.wait()
     for h in range(sz.heads):
         across = [states[r, h].T for r in range(sz.rows)]
-        base = [info[h, at : at + 8, :] for at in range(0, sz.info_rows, 8)]
-        others = {
-            tile: [tails[shift, h, tile * 8 : tile * 8 + 8, :] for shift in range(3)]
-            for tile in masks
-        }
         for cut in range(sz.cuts):
             p, at = h * sz.cuts + cut, cut * sz.cols
             own = [a[at : at + sz.cols] for a in across]
             pieces[p, : sz.state_rows, :] = jnp.concatenate(own, axis=0).astype(BF16)
-            rest = list(base)
-            for tile in masks:
-                for shift in range(3):
-                    rest[tile] = jnp.where(
-                        masks[tile][cut][shift], others[tile][shift], rest[tile]
-                    )
-            pieces[p, sz.state_rows :, :] = jnp.concatenate(rest, axis=0).astype(BF16)
+            for at, value in zip(shared, held[h]):
+                to = sz.state_rows + at
+                pieces[p, to : to + value.shape[0], :] = value
+            for at in range(0, sz.info_rows, 16):
+                if at in shared:
+                    continue
+                rest = []
+                for tile in range(at // 8, min(at + 16, sz.info_rows) // 8):
+                    rows = slice(tile * 8, tile * 8 + 8)
+                    value = info[h, rows, :]
+                    for shift in range(3 if tile in masks else 0):
+                        value = jnp.where(masks[tile][cut][shift], tails[shift, h, rows, :], value)
+                    rest.append(value)
+                rest = jnp.concatenate(rest, axis=0)
+                to = sz.state_rows + at
+                pieces[p, to : to + rest.shape[0], :] = rest.astype(BF16)
 
 
 def route(sz, targets, pick, place, final):

time: 45 us -> 44.8 us (level)
  no operation moved by 1% of the time
where the time goes in v2:
time: 44.8 us; the launch traced here: 44.5 us
  blocking collectives  35.2 us (79%)
  Pallas kernels  5.17 us (12%)
  starting transfers between devices  1.58 us (4%)
  waiting for transfers between devices  1.31 us (3%)
  between operations  0.67 us (1%)
  other arithmetic  0.64 us (1%)
    all_to_all x2, blocking collectives, exchange(): lax.all_to_all(pieces, 'rep', split_axis=0, concat_axis=0, axis_index_gro...  35.2 us
    pallas_call x1, Pallas kernels, local(): call(functools.partial(step_kernel, sz), (shape((n, sz.state_rows + sz.ba...  1.91 us
    pallas_call x1, Pallas kernels, local(): call(functools.partial(pack_kernel, sz), (shape((n, sz.state_rows + sz.in...  1.82 us
    ppermute x1, starting transfers between devices, local(): passed = lax.ppermute(partials[shift].astype(BF16), 'head', pairs)  1.58 us
    ppermute x1, waiting for transfers between devices, local(): passed = lax.ppermute(partials[shift].astype(BF16), 'head', pairs)  1.31 us
    pallas_call x1, Pallas kernels, local(): call(functools.partial(restore_kernel, sz, blocks), (shape(states.shape,...  1.03 us
  transfers between devices with their start and end apart: 1, of which 1 were waited for; matrix products, arithmetic and copies ran while one was open for 0% of the time, Pallas kernels for 2%

profile of v2, /device:TPU:0, one launch (start us, length us, event | category | flops | bytes accessed | tf_op | source)
XLA Modules:
  0.0 44.5 jit_solution(17105240765295981777)
XLA Ops:
  0.6 0.0 copy-start
  0.6 1.8 %pack.1 = (bf16[16,120,128]{2,1,0:T(8,128)(2,1)S(1)}, bf16[6,32,32]{2,1,0:T(8,128)(2,1)S(1)}, bf16[6,32,32]{2,1,0:T(8,128)(2,1)S(1)}, s32[8,32]{1,0:T(8,128)S(1)}, f32[3,4,128]{2,1,0:T(4,128)S(1)}) custom-call(s32[6,32]{1,0:T(8,128)} %refs_0_.1, s32[1,6]{1,0:T(1,128)} %bitcast.12, f32[1,4]{1,0:T(1,128)} %bitcast.14, f32[2,4,6]{2,1,0:T(4,128)} %bitcast.11, ...), custom_call_target="tpu_custom_call" | custom-call | tf_op jit(solution)/shard_map/pack/pallas_call | solution.py:533
  2.5 20.9 %all_to_all.10.came = bf16[16,120,128]{2,1,0:T(8,128)(2,1)S(1)} all-to-all(bf16[16,120,128]{2,1,0:T(8,128)(2,1)S(1)} %get-tuple-element.18), channel_id=1, replica_groups=mesh['rep'=16,'head'=2] {'rep'}, dimensions={0} | all-to-all | bytes 983040 | tf_op jit(solution)/shard_map/all_to_all | solution.py:496
  23.4 1.9 %steps.1 = (bf16[16,72,128]{2,1,0:T(8,128)(2,1)S(1)}, f32[16,512]{1,0:T(8,128)S(1)}) custom-call(f32[3,4,128]{2,1,0:T(4,128)S(1)} %get-tuple-element.15.filters, bf16[6,32,32]{2,1,0:T(8,128)(2,1)S(1)} %get-tuple-element.16.pick, bf16[6,32,32]{2,1,0:T(8,128)(2,1)S(1)} %get-tuple-element.17.place, bf16[16,120,128]{2,1,0:T(8,128)(2,1)S(1)} %all_to_all.10.came, ...), custom_call_target="tpu_custom_call" | custom-call | tf_op jit(solution)/shard_map/steps/pallas_call | solution.py:555
  25.3 14.2 %all_to_all.11.came = bf16[16,72,128]{2,1,0:T(8,128)(2,1)S(1)} all-to-all(bf16[16,72,128]{2,1,0:T(8,128)(2,1)S(1)} %get-tuple-element.21), channel_id=1, replica_groups={{0,16,8,24,2,18,10,26,4,20,12,28,6,22,14,30},{1,17,9,25,3,19,11,27,5,21..., dimensions={0} | all-to-all | bytes 589824 | tf_op jit(solution)/shard_map/all_to_all | solution.py:496
  39.6 0.0 copy-done
  39.6 0.4 project.1
  40.0 1.6 %collective-permute-start = (bf16[6,2,1152]{2,1,0:T(2,128)(2,1)S(1)}, bf16[6,2,1152]{2,1,0:T(2,128)(2,1)S(1)}, u32[]{:S(2)}, u32[]{:S(2)}) collective-permute-start(bf16[6,2,1152]{2,1,0:T(2,128)(2,1)S(1)} %get-tuple-element.24), channel_id=1, source_target_pairs={{0,1},{1,0},{2,3},{3,2},{4,5},{5,4},{6,7},{7,6},{8,9},{9,8},{10,11... | collective-permute-start | bytes 82952 | tf_op jit(solution)/shard_map/ppermute | solution.py:612
  41.6 1.0 %restore.1 = (f32[2,4,128,128]{3,2,1,0:T(8,128)}, f32[6,2,1152]{2,1,0:T(2,128)S(1)}, bf16[3,3,2,512]{3,2,1,0:T(2,128)(2,1)}) custom-call(bf16[16,512]{1,0:T(8,128)(2,1)S(1)} %get-tuple-element.22.gated, bf16[512,2304]{1,0:T(8,128)(2,1)S(1)} %copy-done, bf16[16,72,128]{2,1,0:T(8,128)(2,1)S(1)} %all_to_all.11.came), custom_call_target="tpu_custom_call" | custom-call | tf_op jit(solution)/shard_map/restore/pallas_call | solution.py:588
  42.6 1.3 %collective-permute-done = bf16[6,2,1152]{2,1,0:T(2,128)(2,1)S(1)} collective-permute-done((bf16[6,2,1152]{2,1,0:T(2,128)(2,1)S(1)}, bf16[6,2,1152]{2,1,0:T(2,128)(2,1)S(1)}, u32[]{:S(2)}, u32[]{:S(2)}) %collective-permute-start) | collective-permute-done | bytes 27680 | tf_op jit(solution)/shard_map/ppermute | solution.py:612
  43.9 0.6 %add_convert_fusion = bf16[6,2,1152]{2,1,0:T(2,128)(2,1)} fusion(f32[6,2,1152]{2,1,0:T(2,128)S(1)} %get-tuple-element.23, bf16[6,2,1152]{2,1,0:T(2,128)(2,1)S(1)} %collective-permute-done), kind=kLoop, calls=%fused_computation | loop fusion | flops 41472 | bytes 110592 | tf_op jit(solution)/shard_map/convert_element_type | solution.py:614
Async XLA Ops:
  0.6 38.9 %copy-start = (bf16[512,2304]{1,0:T(8,128)(2,1)S(1)}, bf16[512,2304]{1,0:T(8,128)(2,1)}, u32[]{:S(2)}) copy-start(bf16[512,2304]{1,0:T(8,128)(2,1)} %weight.3) | copy-start | bytes 7077892
  40.0 3.9 %collective-permute-start = (bf16[6,2,1152]{2,1,0:T(2,128)(2,1)S(1)}, bf16[6,2,1152]{2,1,0:T(2,128)(2,1)S(1)}, u32[]{:S(2)}, u32[]{:S(2)}) collective-permute-start(bf16[6,2,1152]{2,1,0:T(2,128)(2,1)S(1)} %get-tuple-element.24), channel_id=1, source_target_pairs={{0,1},{1,0},{2,3},{3,2},{4,5},{5,4},{6,7},{7,6},{8,9},{9,8},{10,11... | collective-permute-start | bytes 82952 | tf_op jit(solution)/shard_map/ppermute | solution.py:612

commit v3 on v2

--- a/solution.py
+++ b/solution.py
@@ -180,7 +180,7 @@
     for h in range(sz.heads):
         across = [states[r, h].T for r in range(sz.rows)]
         for cut in range(sz.cuts):
-            p, at = h * sz.cuts + cut, cut * sz.cols
+            p, at = sz.place_of[h * sz.cuts + cut], cut * sz.cols
             own = [a[at : at + sz.cols] for a in across]
             pieces[p, : sz.state_rows, :] = jnp.concatenate(own, axis=0).astype(BF16)
             for at, value in zip(shared, held[h]):
@@ -223,17 +223,27 @@
     final[...] = (places + 0.5).astype(jnp.int32)
 
 
+def over_blocks(sz, value):
+    step = sz.cols
+    while step < sz.dk:
+        value = value + pltpu.roll(value, step, 1)
+        step *= 2
+    return value
+
+
 def gate_factor(sz, live, gain, gate, factor):
-    channels = sz.heads * sz.dk
-    gains = jnp.concatenate([gain[...]] * sz.heads, axis=1)
-    row = iota((sz.rows, channels), 0)
     factor[...] = jnp.zeros(factor.shape, F32)
+    row = iota((sz.read_rows, sz.dk), 0)
+    alive = row < 0
     for t in range(sz.steps):
-        gates = gains / (1.0 + jnp.exp(-gate[t].astype(F32)))
-        gates = jnp.where(row < live[:, t : t + 1], gates, 0.0)
         for r in range(sz.rows):
             at = sz.read_at(t, r)
-            factor[at : at + 1, :] = gates[r : r + 1]
+            factor[at : at + 1, :] = gate[t, r : r + 1].astype(F32)
+            alive = alive | ((row == at) & (r < live[:, t : t + 1]))
+    for h in range(sz.heads):
+        lanes = slice(h * sz.dk, (h + 1) * sz.dk)
+        gates = gain[...] / (1.0 + jnp.exp(-factor[:, lanes]))
+        factor[:, lanes] = jnp.where(alive, gates, 0.0)
 
 
 def step_kernel(sz, filters, pick, place, came, *refs):
@@ -249,7 +259,7 @@
     cut = lax.rem(mine, sz.cuts)
     stride = sz.info_rows
     for g in range(count):
-        info[g * stride : (g + 1) * stride, :] = came[g, sz.state_rows :, :].astype(F32)
+        info[g * stride : (g + 1) * stride, :] = came[sz.place_of[g], sz.state_rows :, :].astype(F32)
 
     def gather(index):
         return info[pl.ds(index, n, stride=sz.info_sets), :]
@@ -299,10 +309,12 @@
         values.append(active[2])
         strengths.append(strength)
 
-    spread = one_hot(
-        iota((dk, sz.width), 0) == cut * sz.cols + mod(iota((dk, sz.width), 1), sz.cols)
-    )
-    value_cols = dot(jnp.concatenate(values, axis=0).astype(BF16), spread)
+    own_lanes = in_block(sz, (n, dk), cut, 0)
+    wide = sz.width // dk
+    value_cols = []
+    for value in values:
+        value = over_blocks(sz, jnp.where(own_lanes, value, 0.0))
+        value_cols.append(jnp.concatenate([value] * wide, axis=1))
     for copy in copies:
         copy.wait()
     gate_factor(sz, live, gain, gate, factor)
@@ -315,9 +327,9 @@
         for g in range(at // sz.rows, (at + sz.tile) // sz.rows):
             for r in range(sz.rows):
                 if sz.whole_tiles:
-                    block.append(came[g, r * sz.cols : (r + 1) * sz.cols, :])
+                    block.append(came[sz.place_of[g], r * sz.cols : (r + 1) * sz.cols, :])
                 else:
-                    piece = came[g, : sz.state_rows, :].astype(F32)
+                    piece = came[sz.place_of[g], : sz.state_rows, :].astype(F32)
                     block.append(piece[r * sz.cols : (r + 1) * sz.cols])
         seen = dot(
             jnp.concatenate([x[rows] for x in from_state], axis=0).astype(BF16),
@@ -328,7 +340,7 @@
         seen = [seen[i * sz.tile : (i + 1) * sz.tile] for i in range(2 * T)]
         writes = []
         for t in range(T):
-            target = value_cols[t * n + at : t * n + at + sz.tile] - seen[2 * t]
+            target = value_cols[t][rows] - seen[2 * t]
             target = jnp.where(own, target, 0.0)
             for s in range(t):
                 target = target - key_mix[t][s][rows] * writes[s]
@@ -353,17 +365,16 @@
             else:
                 later[pl.ds(pl.multiple_of(to * sz.cols, sz.cols), sz.cols), :] = part
     blocks = [in_block(sz, (n, dk), cut, shift) for shift in range(4)]
-    lanes = cut * sz.cols + mod(iota((sz.width, dk), 0), sz.cols)
-    fold = [
-        one_hot(iota((sz.width, dk), 1) == mod(lanes + shift * sz.quarter, dk))
-        for shift in range(-(-T // sz.back_depth))
-    ]
     placed = [None] * sz.back_depth
     kept = [None] * sz.back_depth
     for index in range(sz.back_sets):
         shift, slot = index // sz.back_depth, index % sz.back_depth
         if index < T:
-            folded = dot(jnp.concatenate(readouts[index], axis=0).astype(BF16), fold[shift])
+            folded = jnp.concatenate(readouts[index], axis=0)
+            folded = functools.reduce(
+                jnp.add, [folded[:, i * dk : (i + 1) * dk] for i in range(wide)]
+            )
+            folded = jnp.where(blocks[shift], over_blocks(sz, folded), 0.0)
             value = dot(place[index], folded.astype(BF16))
             placed[slot] = value if placed[slot] is None else placed[slot] + value
         else:
@@ -492,9 +503,9 @@
     )
 
 
-def exchange(pieces, groups=None):
+def exchange(sz, pieces):
     return lax.all_to_all(
-        pieces, "rep", split_axis=0, concat_axis=0, axis_index_groups=groups, tiled=True
+        pieces, "rep", split_axis=0, concat_axis=0, axis_index_groups=[sz.order], tiled=True
     )
 
 
@@ -550,7 +561,7 @@
         ],
         "pack",
     )(*[in_hbm(x) for x in arguments])
-    came = exchange(pieces)
+    came = exchange(sz, pieces)
     gain = norm_gain.reshape(1, sz.dk)
     stepped, factor = call(
         functools.partial(step_kernel, sz),
@@ -572,7 +583,7 @@
         ],
         "steps",
     )(taps, pick, place, came, final, in_hbm(lives), in_hbm(gain), in_hbm(out_gate))
-    back = exchange(stepped, [sz.order])
+    back = exchange(sz, stepped)
     width = out_weight.shape[1]
     columns = width // head_total
     blocks = head_total if columns % LANES == 0 else 1

time: 44.8 us -> 44.2 us (0.987)
  blocking collectives: 35.2 us -> 34.7 us
    all_to_all x2, blocking collectives: 35.2 us -> 34.7 us  [exchange(): lax.all_to_all(pieces, 'rep', split_axis=0, concat_axis=0, axis_index_gro...]
where the time goes in v3:
time: 44.2 us; the launch traced here: 43.9 us
  blocking collectives  34.7 us (79%)
  Pallas kernels  5.03 us (11%)
  starting transfers between devices  1.58 us (4%)
  waiting for transfers between devices  1.31 us (3%)
  between operations  0.67 us (2%)
  other arithmetic  0.64 us (1%)
    all_to_all x2, blocking collectives, exchange(): lax.all_to_all(pieces, 'rep', split_axis=0, concat_axis=0, axis_index_gro...  34.7 us
    pallas_call x1, Pallas kernels, local(): call(functools.partial(pack_kernel, sz), (shape((n, sz.state_rows + sz.in...  1.82 us
    pallas_call x1, Pallas kernels, local(): call(functools.partial(step_kernel, sz), (shape((n, sz.state_rows + sz.ba...  1.77 us
    ppermute x1, starting transfers between devices, local(): passed = lax.ppermute(partials[shift].astype(BF16), 'head', pairs)  1.58 us
    ppermute x1, waiting for transfers between devices, local(): passed = lax.ppermute(partials[shift].astype(BF16), 'head', pairs)  1.31 us
    pallas_call x1, Pallas kernels, local(): call(functools.partial(restore_kernel, sz, blocks), (shape(states.shape,...  1.03 us
  transfers between devices with their start and end apart: 1, of which 1 were waited for; matrix products, arithmetic and copies ran while one was open for 0% of the time, Pallas kernels for 2%

profile of v3, /device:TPU:0, one launch (start us, length us, event | category | flops | bytes accessed | tf_op | source)
XLA Modules:
  0.0 43.9 jit_solution(4293492582517184655)
XLA Ops:
  0.6 0.0 copy-start
  0.6 1.8 %pack.1 = (bf16[16,120,128]{2,1,0:T(8,128)(2,1)S(1)}, bf16[6,32,32]{2,1,0:T(8,128)(2,1)S(1)}, bf16[6,32,32]{2,1,0:T(8,128)(2,1)S(1)}, s32[8,32]{1,0:T(8,128)S(1)}, f32[3,4,128]{2,1,0:T(4,128)S(1)}) custom-call(s32[6,32]{1,0:T(8,128)} %refs_0_.1, s32[1,6]{1,0:T(1,128)} %bitcast.12, f32[1,4]{1,0:T(1,128)} %bitcast.14, f32[2,4,6]{2,1,0:T(4,128)} %bitcast.11, ...), custom_call_target="tpu_custom_call" | custom-call | tf_op jit(solution)/shard_map/pack/pallas_call | solution.py:544
  2.5 21.7 %all_to_all.10.came = bf16[16,120,128]{2,1,0:T(8,128)(2,1)S(1)} all-to-all(bf16[16,120,128]{2,1,0:T(8,128)(2,1)S(1)} %get-tuple-element.18), channel_id=1, replica_groups={{0,16,8,24,2,18,10,26,4,20,12,28,6,22,14,30},{1,17,9,25,3,19,11,27,5,21..., dimensions={0} | all-to-all | bytes 983040 | tf_op jit(solution)/shard_map/all_to_all | solution.py:507
  24.2 1.8 %steps.1 = (bf16[16,72,128]{2,1,0:T(8,128)(2,1)S(1)}, f32[16,512]{1,0:T(8,128)S(1)}) custom-call(f32[3,4,128]{2,1,0:T(4,128)S(1)} %get-tuple-element.15.filters, bf16[6,32,32]{2,1,0:T(8,128)(2,1)S(1)} %get-tuple-element.16.pick, bf16[6,32,32]{2,1,0:T(8,128)(2,1)S(1)} %get-tuple-element.17.place, bf16[16,120,128]{2,1,0:T(8,128)(2,1)S(1)} %all_to_all.10.came, ...), custom_call_target="tpu_custom_call" | custom-call | tf_op jit(solution)/shard_map/steps/pallas_call | solution.py:566
  26.0 13.0 %all_to_all.11.came = bf16[16,72,128]{2,1,0:T(8,128)(2,1)S(1)} all-to-all(bf16[16,72,128]{2,1,0:T(8,128)(2,1)S(1)} %get-tuple-element.21), channel_id=1, replica_groups={{0,16,8,24,2,18,10,26,4,20,12,28,6,22,14,30},{1,17,9,25,3,19,11,27,5,21..., dimensions={0} | all-to-all | bytes 589824 | tf_op jit(solution)/shard_map/all_to_all | solution.py:507
  39.0 0.0 copy-done
  39.0 0.4 project.1
  39.4 1.6 %collective-permute-start = (bf16[6,2,1152]{2,1,0:T(2,128)(2,1)S(1)}, bf16[6,2,1152]{2,1,0:T(2,128)(2,1)S(1)}, u32[]{:S(2)}, u32[]{:S(2)}) collective-permute-start(bf16[6,2,1152]{2,1,0:T(2,128)(2,1)S(1)} %get-tuple-element.24), channel_id=1, source_target_pairs={{0,1},{1,0},{2,3},{3,2},{4,5},{5,4},{6,7},{7,6},{8,9},{9,8},{10,11... | collective-permute-start | bytes 82952 | tf_op jit(solution)/shard_map/ppermute | solution.py:623
  41.0 1.0 %restore.1 = (f32[2,4,128,128]{3,2,1,0:T(8,128)}, f32[6,2,1152]{2,1,0:T(2,128)S(1)}, bf16[3,3,2,512]{3,2,1,0:T(2,128)(2,1)}) custom-call(bf16[16,512]{1,0:T(8,128)(2,1)S(1)} %get-tuple-element.22.gated, bf16[512,2304]{1,0:T(8,128)(2,1)S(1)} %copy-done, bf16[16,72,128]{2,1,0:T(8,128)(2,1)S(1)} %all_to_all.11.came), custom_call_target="tpu_custom_call" | custom-call | tf_op jit(solution)/shard_map/restore/pallas_call | solution.py:599
  42.0 1.3 %collective-permute-done = bf16[6,2,1152]{2,1,0:T(2,128)(2,1)S(1)} collective-permute-done((bf16[6,2,1152]{2,1,0:T(2,128)(2,1)S(1)}, bf16[6,2,1152]{2,1,0:T(2,128)(2,1)S(1)}, u32[]{:S(2)}, u32[]{:S(2)}) %collective-permute-start) | collective-permute-done | bytes 27680 | tf_op jit(solution)/shard_map/ppermute | solution.py:623
  43.3 0.6 %add_convert_fusion = bf16[6,2,1152]{2,1,0:T(2,128)(2,1)} fusion(f32[6,2,1152]{2,1,0:T(2,128)S(1)} %get-tuple-element.23, bf16[6,2,1152]{2,1,0:T(2,128)(2,1)S(1)} %collective-permute-done), kind=kLoop, calls=%fused_computation | loop fusion | flops 41472 | bytes 110592 | tf_op jit(solution)/shard_map/convert_element_type | solution.py:625
Async XLA Ops:
  0.6 38.3 %copy-start = (bf16[512,2304]{1,0:T(8,128)(2,1)S(1)}, bf16[512,2304]{1,0:T(8,128)(2,1)}, u32[]{:S(2)}) copy-start(bf16[512,2304]{1,0:T(8,128)(2,1)} %weight.3) | copy-start | bytes 7077892
  39.4 3.9 %collective-permute-start = (bf16[6,2,1152]{2,1,0:T(2,128)(2,1)S(1)}, bf16[6,2,1152]{2,1,0:T(2,128)(2,1)S(1)}, u32[]{:S(2)}, u32[]{:S(2)}) collective-permute-start(bf16[6,2,1152]{2,1,0:T(2,128)(2,1)S(1)} %get-tuple-element.24), channel_id=1, source_target_pairs={{0,1},{1,0},{2,3},{3,2},{4,5},{5,4},{6,7},{7,6},{8,9},{9,8},{10,11... | collective-permute-start | bytes 82952 | tf_op jit(solution)/shard_map/ppermute | solution.py:623

commit v4 on v3

--- a/solution.py
+++ b/solution.py
@@ -16,6 +16,10 @@
 
 def round_up(value, multiple):
     return -(-value // multiple) * multiple
+
+
+def power_of_two(value):
+    return value & (value - 1) == 0
 
 
 class Sizes:
@@ -26,7 +30,9 @@
         self.steps = projected.shape[0]
         self.slots = n * self.rows
         self.cuts = n // self.heads
-        far = [*range(0, self.heads, 2), *range(1, self.heads, 2)]
+        far = range(self.heads)
+        if power_of_two(self.heads):
+            far = [h ^ (h >> 1) for h in far]
         self.order = [h * self.cuts + cut for cut in range(self.cuts) for h in far]
         self.place_of = [self.order.index(p) for p in range(n)]
         self.cols = self.dk // self.cuts
@@ -217,7 +223,11 @@
     slot = iota((8, n), 1)
     row, group = mod(slot, sz.rows), quotient(slot, sz.rows)
     head, cut = quotient(group, sz.cuts), mod(group, sz.cuts)
-    far = quotient(head, 2) + mod(head, 2) * ((sz.heads + 1) // 2)
+    far = head
+    step = 1
+    while power_of_two(sz.heads) and step < sz.heads:
+        far = far ^ lax.shift_right_logical(far, jnp.int32(step))
+        step *= 2
     weights = (cut * sz.heads + far) * sz.rows + row
     places = dot(weights.astype(F32).astype(BF16), chain[T - 1])
     final[...] = (places + 0.5).astype(jnp.int32)

time: 44.2 us -> 44.2 us (level)
  no operation moved by 1% of the time
where the time goes in v4:
time: 44.2 us; the launch traced here: 43.9 us
  blocking collectives  34.7 us (79%)
  Pallas kernels  5.02 us (11%)
  starting transfers between devices  1.58 us (4%)
  waiting for transfers between devices  1.31 us (3%)
  between operations  0.67 us (2%)
  other arithmetic  0.64 us (1%)
    all_to_all x2, blocking collectives, exchange(): lax.all_to_all(pieces, 'rep', split_axis=0, concat_axis=0, axis_index_gro...  34.7 us
    pallas_call x1, Pallas kernels, local(): call(functools.partial(pack_kernel, sz), (shape((n, sz.state_rows + sz.in...  1.82 us
    pallas_call x1, Pallas kernels, local(): call(functools.partial(step_kernel, sz), (shape((n, sz.state_rows + sz.ba...  1.77 us
    ppermute x1, starting transfers between devices, local(): passed = lax.ppermute(partials[shift].astype(BF16), 'head', pairs)  1.58 us
    ppermute x1, waiting for transfers between devices, local(): passed = lax.ppermute(partials[shift].astype(BF16), 'head', pairs)  1.31 us
    pallas_call x1, Pallas kernels, local(): call(functools.partial(restore_kernel, sz, blocks), (shape(states.shape,...  1.03 us
  transfers between devices with their start and end apart: 1, of which 1 were waited for; matrix products, arithmetic and copies ran while one was open for 0% of the time, Pallas kernels for 2%

profile of v4, /device:TPU:0, one launch (start us, length us, event | category | flops | bytes accessed | tf_op | source)
XLA Modules:
  0.0 43.9 jit_solution(14494684116159396123)
XLA Ops:
  0.6 0.0 copy-start
  0.6 1.8 %pack.1 = (bf16[16,120,128]{2,1,0:T(8,128)(2,1)S(1)}, bf16[6,32,32]{2,1,0:T(8,128)(2,1)S(1)}, bf16[6,32,32]{2,1,0:T(8,128)(2,1)S(1)}, s32[8,32]{1,0:T(8,128)S(1)}, f32[3,4,128]{2,1,0:T(4,128)S(1)}) custom-call(s32[6,32]{1,0:T(8,128)} %refs_0_.1, s32[1,6]{1,0:T(1,128)} %bitcast.12, f32[1,4]{1,0:T(1,128)} %bitcast.14, f32[2,4,6]{2,1,0:T(4,128)} %bitcast.11, ...), custom_call_target="tpu_custom_call" | custom-call | tf_op jit(solution)/shard_map/pack/pallas_call | solution.py:554
  2.5 21.4 %all_to_all.10.came = bf16[16,120,128]{2,1,0:T(8,128)(2,1)S(1)} all-to-all(bf16[16,120,128]{2,1,0:T(8,128)(2,1)S(1)} %get-tuple-element.18), channel_id=1, replica_groups={{0,8,24,16,2,10,26,18,4,12,28,20,6,14,30,22},{1,9,25,17,3,11,27,19,5,13..., dimensions={0} | all-to-all | bytes 983040 | tf_op jit(solution)/shard_map/all_to_all | solution.py:517
  23.9 1.8 %steps.1 = (bf16[16,72,128]{2,1,0:T(8,128)(2,1)S(1)}, f32[16,512]{1,0:T(8,128)S(1)}) custom-call(f32[3,4,128]{2,1,0:T(4,128)S(1)} %get-tuple-element.15.filters, bf16[6,32,32]{2,1,0:T(8,128)(2,1)S(1)} %get-tuple-element.16.pick, bf16[6,32,32]{2,1,0:T(8,128)(2,1)S(1)} %get-tuple-element.17.place, bf16[16,120,128]{2,1,0:T(8,128)(2,1)S(1)} %all_to_all.10.came, ...), custom_call_target="tpu_custom_call" | custom-call | tf_op jit(solution)/shard_map/steps/pallas_call | solution.py:576
  25.6 13.3 %all_to_all.11.came = bf16[16,72,128]{2,1,0:T(8,128)(2,1)S(1)} all-to-all(bf16[16,72,128]{2,1,0:T(8,128)(2,1)S(1)} %get-tuple-element.21), channel_id=1, replica_groups={{0,8,24,16,2,10,26,18,4,12,28,20,6,14,30,22},{1,9,25,17,3,11,27,19,5,13..., dimensions={0} | all-to-all | bytes 589824 | tf_op jit(solution)/shard_map/all_to_all | solution.py:517
  38.9 0.0 copy-done
  39.0 0.4 project.1
  39.4 1.6 %collective-permute-start = (bf16[6,2,1152]{2,1,0:T(2,128)(2,1)S(1)}, bf16[6,2,1152]{2,1,0:T(2,128)(2,1)S(1)}, u32[]{:S(2)}, u32[]{:S(2)}) collective-permute-start(bf16[6,2,1152]{2,1,0:T(2,128)(2,1)S(1)} %get-tuple-element.24), channel_id=1, source_target_pairs={{0,1},{1,0},{2,3},{3,2},{4,5},{5,4},{6,7},{7,6},{8,9},{9,8},{10,11... | collective-permute-start | bytes 82952 | tf_op jit(solution)/shard_map/ppermute | solution.py:633
  40.9 1.0 %restore.1 = (f32[2,4,128,128]{3,2,1,0:T(8,128)}, f32[6,2,1152]{2,1,0:T(2,128)S(1)}, bf16[3,3,2,512]{3,2,1,0:T(2,128)(2,1)}) custom-call(bf16[16,512]{1,0:T(8,128)(2,1)S(1)} %get-tuple-element.22.gated, bf16[512,2304]{1,0:T(8,128)(2,1)S(1)} %copy-done, bf16[16,72,128]{2,1,0:T(8,128)(2,1)S(1)} %all_to_all.11.came), custom_call_target="tpu_custom_call" | custom-call | tf_op jit(solution)/shard_map/restore/pallas_call | solution.py:609
  42.0 1.3 %collective-permute-done = bf16[6,2,1152]{2,1,0:T(2,128)(2,1)S(1)} collective-permute-done((bf16[6,2,1152]{2,1,0:T(2,128)(2,1)S(1)}, bf16[6,2,1152]{2,1,0:T(2,128)(2,1)S(1)}, u32[]{:S(2)}, u32[]{:S(2)}) %collective-permute-start) | collective-permute-done | bytes 27680 | tf_op jit(solution)/shard_map/ppermute | solution.py:633
  43.3 0.6 %add_convert_fusion = bf16[6,2,1152]{2,1,0:T(2,128)(2,1)} fusion(f32[6,2,1152]{2,1,0:T(2,128)S(1)} %get-tuple-element.23, bf16[6,2,1152]{2,1,0:T(2,128)(2,1)S(1)} %collective-permute-done), kind=kLoop, calls=%fused_computation | loop fusion | flops 41472 | bytes 110592 | tf_op jit(solution)/shard_map/convert_element_type | solution.py:635
Async XLA Ops:
  0.6 38.3 %copy-start = (bf16[512,2304]{1,0:T(8,128)(2,1)S(1)}, bf16[512,2304]{1,0:T(8,128)(2,1)}, u32[]{:S(2)}) copy-start(bf16[512,2304]{1,0:T(8,128)(2,1)} %weight.3) | copy-start | bytes 7077892
  39.4 3.9 %collective-permute-start = (bf16[6,2,1152]{2,1,0:T(2,128)(2,1)S(1)}, bf16[6,2,1152]{2,1,0:T(2,128)(2,1)S(1)}, u32[]{:S(2)}, u32[]{:S(2)}) collective-permute-start(bf16[6,2,1152]{2,1,0:T(2,128)(2,1)S(1)} %get-tuple-element.24), channel_id=1, source_target_pairs={{0,1},{1,0},{2,3},{3,2},{4,5},{5,4},{6,7},{7,6},{8,9},{9,8},{10,11... | collective-permute-start | bytes 82952 | tf_op jit(solution)/shard_map/ppermute | solution.py:633

commit v5 on v4

--- a/solution.py
+++ b/solution.py
@@ -286,9 +286,7 @@
         + [gather_value(T + tap)]
         for tap in range(sz.taps)
     ]
-    reach = jnp.ones((n, dk), F32)
-    keys = []
-    from_state, values, strengths, key_mix, read_mix = [], [], [], [], []
+    active, retains, strengths = [], [], []
     for t in range(T):
         slots = [gather(t * 2 + part) for part in range(2)]
         slots += [gather_value(t), gather(sz.decay_at + t), flags]
@@ -297,7 +295,6 @@
         moved_flags = inputs[sz.parts + 1]
         strength = moved_flags[:, t : t + 1] + moved_flags[:, 32 + t : 33 + t]
         alive = moved_flags[:, 16 + t : 17 + t] > 0.5
-        active = []
         for part in range(sz.parts):
             frames = [window[tap][part] for tap in range(sz.taps)] + [inputs[part]]
             total = frames[0] * weights[part][:1]
@@ -306,18 +303,36 @@
             active.append(total / (1.0 + jnp.exp(-total)))
             for tap in range(sz.taps):
                 window[tap][part] = jnp.where(alive, frames[tap + 1], frames[tap])
-        query, key = (
-            x * lax.rsqrt(jnp.sum(x * x, axis=1, keepdims=True) + EPSILON) for x in active[:2]
-        )
-        retain = jnp.exp(-inputs[sz.parts])
-        reach = reach * retain
-        keys = [k * retain for k in keys]
-        key_mix.append([jnp.sum(key * k, axis=1, keepdims=True) for k in keys])
+        retains.append(jnp.exp(-inputs[sz.parts]))
+        strengths.append(strength)
+
+    ones = jnp.ones((dk, dk), BF16)
+
+    def summed(products):
+        sums = dot(jnp.concatenate([x.astype(BF16) for x in products], axis=0), ones)
+        return [sums[i * n : (i + 1) * n] for i in range(len(products))]
+
+    values = active[2 :: sz.parts]
+    units = [x for i, x in enumerate(active) if i % sz.parts < 2]
+    norms = summed([x * x for x in units])
+    units = [x * lax.rsqrt(norm + EPSILON) for x, norm in zip(units, norms)]
+    reach = jnp.ones((n, dk), F32)
+    keys = []
+    from_state, pairs = [], []
+    for t in range(T):
+        query, key = units[2 * t], units[2 * t + 1]
+        reach = reach * retains[t]
+        keys = [k * retains[t] for k in keys]
+        pairs += [key * k for k in keys]
         keys.append(key)
-        read_mix.append([jnp.sum(query * k, axis=1, keepdims=True) for k in keys])
+        pairs += [query * k for k in keys]
         from_state += [reach * key, reach * query]
-        values.append(active[2])
-        strengths.append(strength)
+    mixes = summed(pairs)
+    key_mix, read_mix = [], []
+    for t in range(T):
+        key_mix.append(mixes[:t])
+        read_mix.append(mixes[t : 2 * t + 1])
+        mixes = mixes[2 * t + 1 :]
 
     own_lanes = in_block(sz, (n, dk), cut, 0)
     wide = sz.width // dk
@@ -331,6 +346,10 @@
     lane_row = quotient(iota((sz.tile, sz.width), 1), sz.cols)
     own = iota((sz.tile, sz.width), 0) == lane_row
     readouts = [[] for _ in range(T)]
+
+    def widen(value):
+        return jnp.concatenate([value] * wide, axis=1)
+
     for at in range(0, n, sz.tile):
         rows = slice(at, at + sz.tile)
         block = []
@@ -353,11 +372,11 @@
             target = value_cols[t][rows] - seen[2 * t]
             target = jnp.where(own, target, 0.0)
             for s in range(t):
-                target = target - key_mix[t][s][rows] * writes[s]
+                target = target - widen(key_mix[t][s][rows]) * writes[s]
             writes.append(strengths[t][rows] * target)
             read = jnp.where(own, seen[2 * t + 1], 0.0)
             for s in range(t + 1):
-                read = read + read_mix[t][s][rows] * writes[s]
+                read = read + widen(read_mix[t][s][rows]) * writes[s]
             readouts[t].append(read * dk ** (-0.5))
         added = dot(
             jnp.concatenate(writes, axis=0).astype(BF16),

time: 44.2 us -> 44.1 us (level)
  no operation moved by 1% of the time
where the time goes in v5:
time: 44.1 us; the launch traced here: 43.8 us
  blocking collectives  34.7 us (79%)
  Pallas kernels  4.87 us (11%)
  starting transfers between devices  1.58 us (4%)
  waiting for transfers between devices  1.31 us (3%)
  between operations  0.67 us (2%)
  other arithmetic  0.64 us (1%)
    all_to_all x2, blocking collectives, exchange(): lax.all_to_all(pieces, 'rep', split_axis=0, concat_axis=0, axis_index_gro...  34.7 us
    pallas_call x1, Pallas kernels, local(): call(functools.partial(pack_kernel, sz), (shape((n, sz.state_rows + sz.in...  1.82 us
    pallas_call x1, Pallas kernels, local(): call(functools.partial(step_kernel, sz), (shape((n, sz.state_rows + sz.ba...  1.61 us
    ppermute x1, starting transfers between devices, local(): passed = lax.ppermute(partials[shift].astype(BF16), 'head', pairs)  1.58 us
    ppermute x1, waiting for transfers between devices, local(): passed = lax.ppermute(partials[shift].astype(BF16), 'head', pairs)  1.31 us
    pallas_call x1, Pallas kernels, local(): call(functools.partial(restore_kernel, sz, blocks), (shape(states.shape,...  1.03 us
  transfers between devices with their start and end apart: 1, of which 1 were waited for; matrix products, arithmetic and copies ran while one was open for 0% of the time, Pallas kernels for 2%

profile of v5, /device:TPU:0, one launch (start us, length us, event | category | flops | bytes accessed | tf_op | source)
XLA Modules:
  0.0 43.8 jit_solution(2785803847693914427)
XLA Ops:
  0.6 0.0 copy-start
  0.6 1.8 %pack.1 = (bf16[16,120,128]{2,1,0:T(8,128)(2,1)S(1)}, bf16[6,32,32]{2,1,0:T(8,128)(2,1)S(1)}, bf16[6,32,32]{2,1,0:T(8,128)(2,1)S(1)}, s32[8,32]{1,0:T(8,128)S(1)}, f32[3,4,128]{2,1,0:T(4,128)S(1)}) custom-call(s32[6,32]{1,0:T(8,128)} %refs_0_.1, s32[1,6]{1,0:T(1,128)} %bitcast.12, f32[1,4]{1,0:T(1,128)} %bitcast.14, f32[2,4,6]{2,1,0:T(4,128)} %bitcast.11, ...), custom_call_target="tpu_custom_call" | custom-call | tf_op jit(solution)/shard_map/pack/pallas_call | solution.py:573
  2.5 21.4 %all_to_all.10.came = bf16[16,120,128]{2,1,0:T(8,128)(2,1)S(1)} all-to-all(bf16[16,120,128]{2,1,0:T(8,128)(2,1)S(1)} %get-tuple-element.18), channel_id=1, replica_groups={{0,8,24,16,2,10,26,18,4,12,28,20,6,14,30,22},{1,9,25,17,3,11,27,19,5,13..., dimensions={0} | all-to-all | bytes 983040 | tf_op jit(solution)/shard_map/all_to_all | solution.py:536
  23.9 1.6 %steps.1 = (bf16[16,72,128]{2,1,0:T(8,128)(2,1)S(1)}, f32[16,512]{1,0:T(8,128)S(1)}) custom-call(f32[3,4,128]{2,1,0:T(4,128)S(1)} %get-tuple-element.15.filters, bf16[6,32,32]{2,1,0:T(8,128)(2,1)S(1)} %get-tuple-element.16.pick, bf16[6,32,32]{2,1,0:T(8,128)(2,1)S(1)} %get-tuple-element.17.place, bf16[16,120,128]{2,1,0:T(8,128)(2,1)S(1)} %all_to_all.10.came, ...), custom_call_target="tpu_custom_call" | custom-call | tf_op jit(solution)/shard_map/steps/pallas_call | solution.py:595
  25.5 13.3 %all_to_all.11.came = bf16[16,72,128]{2,1,0:T(8,128)(2,1)S(1)} all-to-all(bf16[16,72,128]{2,1,0:T(8,128)(2,1)S(1)} %get-tuple-element.21), channel_id=1, replica_groups={{0,8,24,16,2,10,26,18,4,12,28,20,6,14,30,22},{1,9,25,17,3,11,27,19,5,13..., dimensions={0} | all-to-all | bytes 589824 | tf_op jit(solution)/shard_map/all_to_all | solution.py:536
  38.8 0.0 copy-done
  38.8 0.4 project.1
  39.2 1.6 %collective-permute-start = (bf16[6,2,1152]{2,1,0:T(2,128)(2,1)S(1)}, bf16[6,2,1152]{2,1,0:T(2,128)(2,1)S(1)}, u32[]{:S(2)}, u32[]{:S(2)}) collective-permute-start(bf16[6,2,1152]{2,1,0:T(2,128)(2,1)S(1)} %get-tuple-element.24), channel_id=1, source_target_pairs={{0,1},{1,0},{2,3},{3,2},{4,5},{5,4},{6,7},{7,6},{8,9},{9,8},{10,11... | collective-permute-start | bytes 82952 | tf_op jit(solution)/shard_map/ppermute | solution.py:652
  40.8 1.0 %restore.1 = (f32[2,4,128,128]{3,2,1,0:T(8,128)}, f32[6,2,1152]{2,1,0:T(2,128)S(1)}, bf16[3,3,2,512]{3,2,1,0:T(2,128)(2,1)}) custom-call(bf16[16,512]{1,0:T(8,128)(2,1)S(1)} %get-tuple-element.22.gated, bf16[512,2304]{1,0:T(8,128)(2,1)S(1)} %copy-done, bf16[16,72,128]{2,1,0:T(8,128)(2,1)S(1)} %all_to_all.11.came), custom_call_target="tpu_custom_call" | custom-call | tf_op jit(solution)/shard_map/restore/pallas_call | solution.py:628
  41.8 1.3 %collective-permute-done = bf16[6,2,1152]{2,1,0:T(2,128)(2,1)S(1)} collective-permute-done((bf16[6,2,1152]{2,1,0:T(2,128)(2,1)S(1)}, bf16[6,2,1152]{2,1,0:T(2,128)(2,1)S(1)}, u32[]{:S(2)}, u32[]{:S(2)}) %collective-permute-start) | collective-permute-done | bytes 27680 | tf_op jit(solution)/shard_map/ppermute | solution.py:652
  43.1 0.6 %add_convert_fusion = bf16[6,2,1152]{2,1,0:T(2,128)(2,1)} fusion(f32[6,2,1152]{2,1,0:T(2,128)S(1)} %get-tuple-element.23, bf16[6,2,1152]{2,1,0:T(2,128)(2,1)S(1)} %collective-permute-done), kind=kLoop, calls=%fused_computation | loop fusion | flops 41472 | bytes 110592 | tf_op jit(solution)/shard_map/convert_element_type | solution.py:654
Async XLA Ops:
  0.6 38.2 %copy-start = (bf16[512,2304]{1,0:T(8,128)(2,1)S(1)}, bf16[512,2304]{1,0:T(8,128)(2,1)}, u32[]{:S(2)}) copy-start(bf16[512,2304]{1,0:T(8,128)(2,1)} %weight.3) | copy-start | bytes 7077892
  39.2 3.9 %collective-permute-start = (bf16[6,2,1152]{2,1,0:T(2,128)(2,1)S(1)}, bf16[6,2,1152]{2,1,0:T(2,128)(2,1)S(1)}, u32[]{:S(2)}, u32[]{:S(2)}) collective-permute-start(bf16[6,2,1152]{2,1,0:T(2,128)(2,1)S(1)} %get-tuple-element.24), channel_id=1, source_target_pairs={{0,1},{1,0},{2,3},{3,2},{4,5},{5,4},{6,7},{7,6},{8,9},{9,8},{10,11... | collective-permute-start | bytes 82952 | tf_op jit(solution)/shard_map/ppermute | solution.py:652

commit v6 on v5

--- a/solution.py
+++ b/solution.py
@@ -94,8 +94,8 @@
 def pack_kernel(sz, *refs):
     count = 8
     sources, states_hbm = refs[:count], refs[count]
-    pieces, pick, place, final, taps = refs[count + 1 : count + 6]
-    scratch = refs[count + 6 :]
+    pieces, place, taps = refs[count + 1 : count + 4]
+    scratch = refs[count + 4 :]
     targets, live, rate, beta, proj, hist, decay, filters, states = scratch[: count + 1]
     info, tails, strengths, in_sems = scratch[count + 1 :]
     copies = []
@@ -111,7 +111,6 @@
             start(states_hbm.at[r, h], states.at[r, h])
     for copy in copies[:count]:
         copy.wait()
-    route(sz, targets, pick, place, final)
     own_head = lax.axis_index("rep") // sz.cuts
     head_lanes = pl.ds(pl.multiple_of(own_head * sz.dk, sz.dk), sz.dk)
     for part in range(sz.parts):
@@ -183,6 +182,7 @@
     held = [[info[h, at : at + 16, :].astype(BF16) for at in shared] for h in range(sz.heads)]
     for copy in copies[count:]:
         copy.wait()
+    route(sz, targets, place)
     for h in range(sz.heads):
         across = [states[r, h].T for r in range(sz.rows)]
         for cut in range(sz.cuts):
@@ -207,7 +207,7 @@
                 pieces[p, to : to + rest.shape[0], :] = rest.astype(BF16)
 
 
-def route(sz, targets, pick, place, final):
+def route(sz, targets, place):
     n, T = sz.slots, sz.steps
     steps = [one_hot(iota((n, n), 0) == targets[t : t + 1, :]) for t in range(T)]
     chain = [steps[0]]
@@ -219,8 +219,10 @@
             chain.append(dot(steps[t], chain[t - 1]).astype(BF16))
     for t in range(T):
         place[t] = chain[t]
-        pick[t] = chain[t].astype(F32).T.astype(BF16)
-    slot = iota((8, n), 1)
+
+
+def final_places(sz, place):
+    slot = iota((8, sz.slots), 1)
     row, group = mod(slot, sz.rows), quotient(slot, sz.rows)
     head, cut = quotient(group, sz.cuts), mod(group, sz.cuts)
     far = head
@@ -229,8 +231,8 @@
         far = far ^ lax.shift_right_logical(far, jnp.int32(step))
         step *= 2
     weights = (cut * sz.heads + far) * sz.rows + row
-    places = dot(weights.astype(F32).astype(BF16), chain[T - 1])
-    final[...] = (places + 0.5).astype(jnp.int32)
+    places = dot(weights.astype(F32).astype(BF16), place)
+    return (places + 0.5).astype(jnp.int32)
 
 
 def over_blocks(sz, value):
@@ -256,14 +258,18 @@
         factor[:, lanes] = jnp.where(alive, gates, 0.0)
 
 
-def step_kernel(sz, filters, pick, place, came, *refs):
+def step_kernel(sz, filters, place, came, *refs):
     count = sz.groups
-    sources, sent, factor, scratch = refs[:4], refs[4], refs[5], refs[6:]
-    scalars, live, gain, gate, info, later, back, sems = scratch
+    sources, sent, factor, scratch = refs[:3], refs[3], refs[4], refs[5:]
+    live, gain, gate, final, scalars, info, later, back, sems = scratch
     copies = []
-    for i, (source, target) in enumerate(zip(sources, scratch)):
-        copies.append(pltpu.make_async_copy(source, target, sems.at[i]))
+
+    def start(source, target):
+        copies.append(pltpu.make_async_copy(source, target, sems.at[len(copies)]))
         copies[-1].start()
+
+    for source, target in zip(sources, scratch):
+        start(source, target)
     n, dk, T = sz.slots, sz.dk, sz.steps
     mine = lax.axis_index("rep")
     cut = lax.rem(mine, sz.cuts)
@@ -279,6 +285,8 @@
         shift = index // sz.value_depth
         return pltpu.roll(value, dk - shift * sz.quarter, 1) if shift else value
 
+    final[...] = final_places(sz, place[T - 1])
+    start(final, scalars)
     weights = [filters[part] for part in range(sz.parts)]
     flags = gather(sz.flag_at)
     window = [
@@ -290,7 +298,7 @@
     for t in range(T):
         slots = [gather(t * 2 + part) for part in range(2)]
         slots += [gather_value(t), gather(sz.decay_at + t), flags]
-        moved = dot(pick[t], jnp.concatenate(slots, axis=1).astype(BF16))
+        moved = dot(place[t], jnp.concatenate(slots, axis=1).astype(BF16), 0, 0)
         inputs = [moved[:, i * dk : (i + 1) * dk] for i in range(sz.parts + 2)]
         moved_flags = inputs[sz.parts + 1]
         strength = moved_flags[:, t : t + 1] + moved_flags[:, 32 + t : 33 + t]
@@ -569,18 +577,15 @@
         conv_weight.transpose(1, 0, 2),
         states,
     )
-    routes = shape((sz.steps, sz.slots, sz.slots), BF16)
-    pieces, pick, place, final, taps = call(
+    pieces, place, taps = call(
         functools.partial(pack_kernel, sz),
         (
             shape((n, sz.state_rows + sz.info_rows, sz.dk), BF16),
-            routes,
-            routes,
-            shape((8, sz.slots), jnp.int32),
+            shape((sz.steps, sz.slots, sz.slots), BF16),
             shape((sz.parts, sz.taps + 1, sz.dk), F32),
         ),
         [anywhere()] * len(arguments),
-        (vmem(),) * 5,
+        (vmem(),) * 3,
         [pltpu.VMEM(x.shape, x.dtype) for x in arguments]
         + [
             pltpu.VMEM((sz.heads, sz.info_rows, sz.dk), F32),
@@ -598,20 +603,21 @@
             shape((n, sz.state_rows + sz.back_rows, sz.dk), BF16),
             shape((sz.read_rows, channels), F32),
         ),
-        [vmem()] * 4 + [anywhere()] * 4,
+        [vmem()] * 3 + [anywhere()] * 3,
         (vmem(), vmem()),
         [
-            pltpu.SMEM((8, sz.slots), jnp.int32),
             pltpu.VMEM(lives.shape, lives.dtype),
             pltpu.VMEM(gain.shape, F32),
             pltpu.VMEM(out_gate.shape, BF16),
+            pltpu.VMEM((8, sz.slots), jnp.int32),
+            pltpu.SMEM((8, sz.slots), jnp.int32),
             pltpu.VMEM((n * sz.info_rows, sz.dk), F32),
             pltpu.VMEM((8 if sz.whole_tiles else n * sz.state_rows, sz.dk), F32),
             pltpu.VMEM((n * sz.back_rows, sz.dk), F32),
             pltpu.SemaphoreType.DMA((4,)),
         ],
         "steps",
-    )(taps, pick, place, came, final, in_hbm(lives), in_hbm(gain), in_hbm(out_gate))
+    )(taps, place, came, in_hbm(lives), in_hbm(gain), in_hbm(out_gate))
     back = exchange(sz, stepped)
     width = out_weight.shape[1]
     columns = width // head_total

time: 44.1 us -> 44.6 us (1.011)
  Pallas kernels: 4.87 us -> 5.36 us
where the time goes in v6:
time: 44.6 us; the launch traced here: 44.3 us
  blocking collectives  34.7 us (78%)
  Pallas kernels  5.36 us (12%)
  starting transfers between devices  1.58 us (4%)
  waiting for transfers between devices  1.31 us (3%)
  between operations  0.67 us (2%)
  other arithmetic  0.64 us (1%)
    all_to_all x2, blocking collectives, exchange(): lax.all_to_all(pieces, 'rep', split_axis=0, concat_axis=0, axis_index_gro...  34.7 us
    pallas_call x1, Pallas kernels, local(): call(functools.partial(step_kernel, sz), (shape((n, sz.state_rows + sz.ba...  2.06 us
    pallas_call x1, Pallas kernels, local(): call(functools.partial(pack_kernel, sz), (shape((n, sz.state_rows + sz.in...  1.86 us
    ppermute x1, starting transfers between devices, local(): passed = lax.ppermute(partials[shift].astype(BF16), 'head', pairs)  1.58 us
    ppermute x1, waiting for transfers between devices, local(): passed = lax.ppermute(partials[shift].astype(BF16), 'head', pairs)  1.31 us
    pallas_call x1, Pallas kernels, local(): call(functools.partial(restore_kernel, sz, blocks), (shape(states.shape,...  1.03 us
  transfers between devices with their start and end apart: 1, of which 1 were waited for; matrix products, arithmetic and copies ran while one was open for 0% of the time, Pallas kernels for 2%

profile of v6, /device:TPU:0, one launch (start us, length us, event | category | flops | bytes accessed | tf_op | source)
XLA Modules:
  0.0 44.3 jit_solution(3586410499058978541)
XLA Ops:
  0.6 0.0 copy-start
  0.6 1.9 %pack.1 = (bf16[16,120,128]{2,1,0:T(8,128)(2,1)S(1)}, bf16[6,32,32]{2,1,0:T(8,128)(2,1)S(1)}, f32[3,4,128]{2,1,0:T(4,128)S(1)}) custom-call(s32[6,32]{1,0:T(8,128)} %refs_0_.1, s32[1,6]{1,0:T(1,128)} %bitcast.12, f32[1,4]{1,0:T(1,128)} %bitcast.14, f32[2,4,6]{2,1,0:T(4,128)} %bitcast.11, bf16[6,3,2,512]{3,2,1,0:T(2,128)(2,1)} %bitcast.8, ...), custom_call_target="tpu_custom_call" | custom-call | tf_op jit(solution)/shard_map/pack/pallas_call | solution.py:580
  2.5 21.4 %all_to_all.10.came = bf16[16,120,128]{2,1,0:T(8,128)(2,1)S(1)} all-to-all(bf16[16,120,128]{2,1,0:T(8,128)(2,1)S(1)} %get-tuple-element.15), channel_id=1, replica_groups={{0,8,24,16,2,10,26,18,4,12,28,20,6,14,30,22},{1,9,25,17,3,11,27,19,5,13..., dimensions={0} | all-to-all | bytes 983040 | tf_op jit(solution)/shard_map/all_to_all | solution.py:544
  23.9 2.1 %steps.1 = (bf16[16,72,128]{2,1,0:T(8,128)(2,1)S(1)}, f32[16,512]{1,0:T(8,128)S(1)}) custom-call(f32[3,4,128]{2,1,0:T(4,128)S(1)} %get-tuple-element.13.filters, bf16[6,32,32]{2,1,0:T(8,128)(2,1)S(1)} %get-tuple-element.14.place, bf16[16,120,128]{2,1,0:T(8,128)(2,1)S(1)} %all_to_all.10.came, s32[1,6]{1,0:T(1,128)} %bitcast.13, f32[1,128]{1,0:T(1,128)} %bitcast.15, ...), custom_call_target="tpu_custom_call" | custom-call | tf_op jit(solution)/shard_map/steps/pallas_call | solution.py:600
  26.0 13.3 %all_to_all.11.came = bf16[16,72,128]{2,1,0:T(8,128)(2,1)S(1)} all-to-all(bf16[16,72,128]{2,1,0:T(8,128)(2,1)S(1)} %get-tuple-element.17), channel_id=1, replica_groups={{0,8,24,16,2,10,26,18,4,12,28,20,6,14,30,22},{1,9,25,17,3,11,27,19,5,13..., dimensions={0} | all-to-all | bytes 589824 | tf_op jit(solution)/shard_map/all_to_all | solution.py:544
  39.3 0.0 copy-done
  39.3 0.4 project.1
  39.7 1.6 %collective-permute-start = (bf16[6,2,1152]{2,1,0:T(2,128)(2,1)S(1)}, bf16[6,2,1152]{2,1,0:T(2,128)(2,1)S(1)}, u32[]{:S(2)}, u32[]{:S(2)}) collective-permute-start(bf16[6,2,1152]{2,1,0:T(2,128)(2,1)S(1)} %get-tuple-element.20), channel_id=1, source_target_pairs={{0,1},{1,0},{2,3},{3,2},{4,5},{5,4},{6,7},{7,6},{8,9},{9,8},{10,11... | collective-permute-start | bytes 82952 | tf_op jit(solution)/shard_map/ppermute | solution.py:658
  41.3 1.0 %restore.1 = (f32[2,4,128,128]{3,2,1,0:T(8,128)}, f32[6,2,1152]{2,1,0:T(2,128)S(1)}, bf16[3,3,2,512]{3,2,1,0:T(2,128)(2,1)}) custom-call(bf16[16,512]{1,0:T(8,128)(2,1)S(1)} %get-tuple-element.18.gated, bf16[512,2304]{1,0:T(8,128)(2,1)S(1)} %copy-done, bf16[16,72,128]{2,1,0:T(8,128)(2,1)S(1)} %all_to_all.11.came), custom_call_target="tpu_custom_call" | custom-call | tf_op jit(solution)/shard_map/restore/pallas_call | solution.py:634
  42.3 1.3 %collective-permute-done = bf16[6,2,1152]{2,1,0:T(2,128)(2,1)S(1)} collective-permute-done((bf16[6,2,1152]{2,1,0:T(2,128)(2,1)S(1)}, bf16[6,2,1152]{2,1,0:T(2,128)(2,1)S(1)}, u32[]{:S(2)}, u32[]{:S(2)}) %collective-permute-start) | collective-permute-done | bytes 27680 | tf_op jit(solution)/shard_map/ppermute | solution.py:658
  43.6 0.6 %add_convert_fusion = bf16[6,2,1152]{2,1,0:T(2,128)(2,1)} fusion(f32[6,2,1152]{2,1,0:T(2,128)S(1)} %get-tuple-element.19, bf16[6,2,1152]{2,1,0:T(2,128)(2,1)S(1)} %collective-permute-done), kind=kLoop, calls=%fused_computation | loop fusion | flops 41472 | bytes 110592 | tf_op jit(solution)/shard_map/convert_element_type | solution.py:660
Async XLA Ops:
  0.6 38.7 %copy-start = (bf16[512,2304]{1,0:T(8,128)(2,1)S(1)}, bf16[512,2304]{1,0:T(8,128)(2,1)}, u32[]{:S(2)}) copy-start(bf16[512,2304]{1,0:T(8,128)(2,1)} %weight.3) | copy-start | bytes 7077892
  39.7 3.9 %collective-permute-start = (bf16[6,2,1152]{2,1,0:T(2,128)(2,1)S(1)}, bf16[6,2,1152]{2,1,0:T(2,128)(2,1)S(1)}, u32[]{:S(2)}, u32[]{:S(2)}) collective-permute-start(bf16[6,2,1152]{2,1,0:T(2,128)(2,1)S(1)} %get-tuple-element.20), channel_id=1, source_target_pairs={{0,1},{1,0},{2,3},{3,2},{4,5},{5,4},{6,7},{7,6},{8,9},{9,8},{10,11... | collective-permute-start | bytes 82952 | tf_op jit(solution)/shard_map/ppermute | solution.py:658

commit v7 on v5

--- a/solution.py
+++ b/solution.py
@@ -106,8 +106,8 @@
 
     for source, target in zip(sources, scratch):
         start(source, target)
-    for r in range(sz.rows):
-        for h in range(sz.heads):
+    for h in range(sz.heads):
+        for r in range(sz.rows):
             start(states_hbm.at[r, h], states.at[r, h])
     for copy in copies[:count]:
         copy.wait()
@@ -181,9 +181,9 @@
         at for at in range(0, sz.info_rows, 16) if at // 8 not in masks and at // 8 + 1 not in masks
     ]
     held = [[info[h, at : at + 16, :].astype(BF16) for at in shared] for h in range(sz.heads)]
-    for copy in copies[count:]:
-        copy.wait()
     for h in range(sz.heads):
+        for copy in copies[count + h * sz.rows :][: sz.rows]:
+            copy.wait()
         across = [states[r, h].T for r in range(sz.rows)]
         for cut in range(sz.cuts):
             p, at = sz.place_of[h * sz.cuts + cut], cut * sz.cols

time: 44.1 us -> 44.3 us (level)
  no operation moved by 1% of the time
where the time goes in v7:
time: 44.3 us; the launch traced here: 44 us
  blocking collectives  34.7 us (78%)
  Pallas kernels  5.14 us (12%)
  starting transfers between devices  1.58 us (4%)
  waiting for transfers between devices  1.31 us (3%)
  between operations  0.67 us (2%)
  other arithmetic  0.64 us (1%)
    all_to_all x2, blocking collectives, exchange(): lax.all_to_all(pieces, 'rep', split_axis=0, concat_axis=0, axis_index_gro...  34.7 us
    pallas_call x1, Pallas kernels, local(): call(functools.partial(pack_kernel, sz), (shape((n, sz.state_rows + sz.in...  2.09 us
    pallas_call x1, Pallas kernels, local(): call(functools.partial(step_kernel, sz), (shape((n, sz.state_rows + sz.ba...  1.61 us
    ppermute x1, starting transfers between devices, local(): passed = lax.ppermute(partials[shift].astype(BF16), 'head', pairs)  1.58 us
    ppermute x1, waiting for transfers between devices, local(): passed = lax.ppermute(partials[shift].astype(BF16), 'head', pairs)  1.31 us
    pallas_call x1, Pallas kernels, local(): call(functools.partial(restore_kernel, sz, blocks), (shape(states.shape,...  1.03 us
  transfers between devices with their start and end apart: 1, of which 1 were waited for; matrix products, arithmetic and copies ran while one was open for 0% of the time, Pallas kernels for 2%

profile of v7, /device:TPU:0, one launch (start us, length us, event | category | flops | bytes accessed | tf_op | source)
XLA Modules:
  0.0 44.0 jit_solution(14724832502198985793)
XLA Ops:
  0.6 0.0 copy-start
  0.6 2.1 %pack.1 = (bf16[16,120,128]{2,1,0:T(8,128)(2,1)S(1)}, bf16[6,32,32]{2,1,0:T(8,128)(2,1)S(1)}, bf16[6,32,32]{2,1,0:T(8,128)(2,1)S(1)}, s32[8,32]{1,0:T(8,128)S(1)}, f32[3,4,128]{2,1,0:T(4,128)S(1)}) custom-call(s32[6,32]{1,0:T(8,128)} %refs_0_.1, s32[1,6]{1,0:T(1,128)} %bitcast.12, f32[1,4]{1,0:T(1,128)} %bitcast.14, f32[2,4,6]{2,1,0:T(4,128)} %bitcast.11, ...), custom_call_target="tpu_custom_call" | custom-call | tf_op jit(solution)/shard_map/pack/pallas_call | solution.py:573
  2.7 21.4 %all_to_all.10.came = bf16[16,120,128]{2,1,0:T(8,128)(2,1)S(1)} all-to-all(bf16[16,120,128]{2,1,0:T(8,128)(2,1)S(1)} %get-tuple-element.18), channel_id=1, replica_groups={{0,8,24,16,2,10,26,18,4,12,28,20,6,14,30,22},{1,9,25,17,3,11,27,19,5,13..., dimensions={0} | all-to-all | bytes 983040 | tf_op jit(solution)/shard_map/all_to_all | solution.py:536
  24.1 1.6 %steps.1 = (bf16[16,72,128]{2,1,0:T(8,128)(2,1)S(1)}, f32[16,512]{1,0:T(8,128)S(1)}) custom-call(f32[3,4,128]{2,1,0:T(4,128)S(1)} %get-tuple-element.15.filters, bf16[6,32,32]{2,1,0:T(8,128)(2,1)S(1)} %get-tuple-element.16.pick, bf16[6,32,32]{2,1,0:T(8,128)(2,1)S(1)} %get-tuple-element.17.place, bf16[16,120,128]{2,1,0:T(8,128)(2,1)S(1)} %all_to_all.10.came, ...), custom_call_target="tpu_custom_call" | custom-call | tf_op jit(solution)/shard_map/steps/pallas_call | solution.py:595
  25.7 13.3 %all_to_all.11.came = bf16[16,72,128]{2,1,0:T(8,128)(2,1)S(1)} all-to-all(bf16[16,72,128]{2,1,0:T(8,128)(2,1)S(1)} %get-tuple-element.21), channel_id=1, replica_groups={{0,8,24,16,2,10,26,18,4,12,28,20,6,14,30,22},{1,9,25,17,3,11,27,19,5,13..., dimensions={0} | all-to-all | bytes 589824 | tf_op jit(solution)/shard_map/all_to_all | solution.py:536
  39.1 0.0 copy-done
  39.1 0.4 project.1
  39.5 1.6 %collective-permute-start = (bf16[6,2,1152]{2,1,0:T(2,128)(2,1)S(1)}, bf16[6,2,1152]{2,1,0:T(2,128)(2,1)S(1)}, u32[]{:S(2)}, u32[]{:S(2)}) collective-permute-start(bf16[6,2,1152]{2,1,0:T(2,128)(2,1)S(1)} %get-tuple-element.24), channel_id=1, source_target_pairs={{0,1},{1,0},{2,3},{3,2},{4,5},{5,4},{6,7},{7,6},{8,9},{9,8},{10,11... | collective-permute-start | bytes 82952 | tf_op jit(solution)/shard_map/ppermute | solution.py:652
  41.1 1.0 %restore.1 = (f32[2,4,128,128]{3,2,1,0:T(8,128)}, f32[6,2,1152]{2,1,0:T(2,128)S(1)}, bf16[3,3,2,512]{3,2,1,0:T(2,128)(2,1)}) custom-call(bf16[16,512]{1,0:T(8,128)(2,1)S(1)} %get-tuple-element.22.gated, bf16[512,2304]{1,0:T(8,128)(2,1)S(1)} %copy-done, bf16[16,72,128]{2,1,0:T(8,128)(2,1)S(1)} %all_to_all.11.came), custom_call_target="tpu_custom_call" | custom-call | tf_op jit(solution)/shard_map/restore/pallas_call | solution.py:628
  42.1 1.3 %collective-permute-done = bf16[6,2,1152]{2,1,0:T(2,128)(2,1)S(1)} collective-permute-done((bf16[6,2,1152]{2,1,0:T(2,128)(2,1)S(1)}, bf16[6,2,1152]{2,1,0:T(2,128)(2,1)S(1)}, u32[]{:S(2)}, u32[]{:S(2)}) %collective-permute-start) | collective-permute-done | bytes 27680 | tf_op jit(solution)/shard_map/ppermute | solution.py:652
  43.4 0.6 %add_convert_fusion = bf16[6,2,1152]{2,1,0:T(2,128)(2,1)} fusion(f32[6,2,1152]{2,1,0:T(2,128)S(1)} %get-tuple-element.23, bf16[6,2,1152]{2,1,0:T(2,128)(2,1)S(1)} %collective-permute-done), kind=kLoop, calls=%fused_computation | loop fusion | flops 41472 | bytes 110592 | tf_op jit(solution)/shard_map/convert_element_type | solution.py:654
Async XLA Ops:
  0.6 38.4 %copy-start = (bf16[512,2304]{1,0:T(8,128)(2,1)S(1)}, bf16[512,2304]{1,0:T(8,128)(2,1)}, u32[]{:S(2)}) copy-start(bf16[512,2304]{1,0:T(8,128)(2,1)} %weight.3) | copy-start | bytes 7077892
  39.5 3.9 %collective-permute-start = (bf16[6,2,1152]{2,1,0:T(2,128)(2,1)S(1)}, bf16[6,2,1152]{2,1,0:T(2,128)(2,1)S(1)}, u32[]{:S(2)}, u32[]{:S(2)}) collective-permute-start(bf16[6,2,1152]{2,1,0:T(2,128)(2,1)S(1)} %get-tuple-element.24), channel_id=1, source_target_pairs={{0,1},{1,0},{2,3},{3,2},{4,5},{5,4},{6,7},{7,6},{8,9},{9,8},{10,11... | collective-permute-start | bytes 82952 | tf_op jit(solution)/shard_map/ppermute | solution.py:652

commit v8 on v5

--- a/solution.py
+++ b/solution.py
@@ -106,9 +106,7 @@
 
     for source, target in zip(sources, scratch):
         start(source, target)
-    for r in range(sz.rows):
-        for h in range(sz.heads):
-            start(states_hbm.at[r, h], states.at[r, h])
+    start(states_hbm, states)
     for copy in copies[:count]:
         copy.wait()
     route(sz, targets, pick, place, final)
@@ -300,7 +298,10 @@
             total = frames[0] * weights[part][:1]
             for j in range(1, sz.taps + 1):
                 total = total + frames[j] * weights[part][j : j + 1]
-            active.append(total / (1.0 + jnp.exp(-total)))
+            below = 1.0 + jnp.exp(-total)
+            inverse = pltpu.reciprocal(below, approx=True)
+            inverse = inverse * (2.0 - below * inverse)
+            active.append(total * inverse)
             for tap in range(sz.taps):
                 window[tap][part] = jnp.where(alive, frames[tap + 1], frames[tap])
         retains.append(jnp.exp(-inputs[sz.parts]))
@@ -586,7 +587,7 @@
             pltpu.VMEM((sz.heads, sz.info_rows, sz.dk), F32),
             pltpu.VMEM((3, sz.heads, sz.info_rows, sz.dk), F32),
             pltpu.VMEM((sz.heads, sz.dk), F32),
-            pltpu.SemaphoreType.DMA((len(arguments) - 1 + sz.rows * sz.heads,)),
+            pltpu.SemaphoreType.DMA((len(arguments),)),
         ],
         "pack",
     )(*[in_hbm(x) for x in arguments])

time: 44.1 us -> 44.3 us (level)
  no operation moved by 1% of the time
where the time goes in v8:
time: 44.3 us; the launch traced here: 44 us
  blocking collectives  34.7 us (78%)
  Pallas kernels  5.13 us (12%)
  starting transfers between devices  1.58 us (4%)
  waiting for transfers between devices  1.31 us (3%)
  between operations  0.67 us (2%)
  other arithmetic  0.64 us (1%)
    all_to_all x2, blocking collectives, exchange(): lax.all_to_all(pieces, 'rep', split_axis=0, concat_axis=0, axis_index_gro...  34.7 us
    pallas_call x1, Pallas kernels, local(): call(functools.partial(step_kernel, sz), (shape((n, sz.state_rows + sz.ba...  1.94 us
    pallas_call x1, Pallas kernels, local(): call(functools.partial(pack_kernel, sz), (shape((n, sz.state_rows + sz.in...  1.75 us
    ppermute x1, starting transfers between devices, local(): passed = lax.ppermute(partials[shift].astype(BF16), 'head', pairs)  1.58 us
    ppermute x1, waiting for transfers between devices, local(): passed = lax.ppermute(partials[shift].astype(BF16), 'head', pairs)  1.31 us
    pallas_call x1, Pallas kernels, local(): call(functools.partial(restore_kernel, sz, blocks), (shape(states.shape,...  1.03 us
  transfers between devices with their start and end apart: 1, of which 1 were waited for; matrix products, arithmetic and copies ran while one was open for 0% of the time, Pallas kernels for 2%

profile of v8, /device:TPU:0, one launch (start us, length us, event | category | flops | bytes accessed | tf_op | source)
XLA Modules:
  0.0 44.0 jit_solution(12632104127801300217)
XLA Ops:
  0.6 0.0 copy-start
  0.6 1.7 %pack.1 = (bf16[16,120,128]{2,1,0:T(8,128)(2,1)S(1)}, bf16[6,32,32]{2,1,0:T(8,128)(2,1)S(1)}, bf16[6,32,32]{2,1,0:T(8,128)(2,1)S(1)}, s32[8,32]{1,0:T(8,128)S(1)}, f32[3,4,128]{2,1,0:T(4,128)S(1)}) custom-call(s32[6,32]{1,0:T(8,128)} %refs_0_.1, s32[1,6]{1,0:T(1,128)} %bitcast.12, f32[1,4]{1,0:T(1,128)} %bitcast.14, f32[2,4,6]{2,1,0:T(4,128)} %bitcast.11, ...), custom_call_target="tpu_custom_call" | custom-call | tf_op jit(solution)/shard_map/pack/pallas_call | solution.py:574
  2.4 21.4 %all_to_all.10.came = bf16[16,120,128]{2,1,0:T(8,128)(2,1)S(1)} all-to-all(bf16[16,120,128]{2,1,0:T(8,128)(2,1)S(1)} %get-tuple-element.18), channel_id=1, replica_groups={{0,8,24,16,2,10,26,18,4,12,28,20,6,14,30,22},{1,9,25,17,3,11,27,19,5,13..., dimensions={0} | all-to-all | bytes 983040 | tf_op jit(solution)/shard_map/all_to_all | solution.py:537
  23.8 1.9 %steps.1 = (bf16[16,72,128]{2,1,0:T(8,128)(2,1)S(1)}, f32[16,512]{1,0:T(8,128)S(1)}) custom-call(f32[3,4,128]{2,1,0:T(4,128)S(1)} %get-tuple-element.15.filters, bf16[6,32,32]{2,1,0:T(8,128)(2,1)S(1)} %get-tuple-element.16.pick, bf16[6,32,32]{2,1,0:T(8,128)(2,1)S(1)} %get-tuple-element.17.place, bf16[16,120,128]{2,1,0:T(8,128)(2,1)S(1)} %all_to_all.10.came, ...), custom_call_target="tpu_custom_call" | custom-call | tf_op jit(solution)/shard_map/steps/pallas_call | solution.py:596
  25.7 13.3 %all_to_all.11.came = bf16[16,72,128]{2,1,0:T(8,128)(2,1)S(1)} all-to-all(bf16[16,72,128]{2,1,0:T(8,128)(2,1)S(1)} %get-tuple-element.21), channel_id=1, replica_groups={{0,8,24,16,2,10,26,18,4,12,28,20,6,14,30,22},{1,9,25,17,3,11,27,19,5,13..., dimensions={0} | all-to-all | bytes 589824 | tf_op jit(solution)/shard_map/all_to_all | solution.py:537
  39.1 0.0 copy-done
  39.1 0.4 project.1
  39.5 1.6 %collective-permute-start = (bf16[6,2,1152]{2,1,0:T(2,128)(2,1)S(1)}, bf16[6,2,1152]{2,1,0:T(2,128)(2,1)S(1)}, u32[]{:S(2)}, u32[]{:S(2)}) collective-permute-start(bf16[6,2,1152]{2,1,0:T(2,128)(2,1)S(1)} %get-tuple-element.24), channel_id=1, source_target_pairs={{0,1},{1,0},{2,3},{3,2},{4,5},{5,4},{6,7},{7,6},{8,9},{9,8},{10,11... | collective-permute-start | bytes 82952 | tf_op jit(solution)/shard_map/ppermute | solution.py:653
  41.0 1.0 %restore.1 = (f32[2,4,128,128]{3,2,1,0:T(8,128)}, f32[6,2,1152]{2,1,0:T(2,128)S(1)}, bf16[3,3,2,512]{3,2,1,0:T(2,128)(2,1)}) custom-call(bf16[16,512]{1,0:T(8,128)(2,1)S(1)} %get-tuple-element.22.gated, bf16[512,2304]{1,0:T(8,128)(2,1)S(1)} %copy-done, bf16[16,72,128]{2,1,0:T(8,128)(2,1)S(1)} %all_to_all.11.came), custom_call_target="tpu_custom_call" | custom-call | tf_op jit(solution)/shard_map/restore/pallas_call | solution.py:629
  42.1 1.3 %collective-permute-done = bf16[6,2,1152]{2,1,0:T(2,128)(2,1)S(1)} collective-permute-done((bf16[6,2,1152]{2,1,0:T(2,128)(2,1)S(1)}, bf16[6,2,1152]{2,1,0:T(2,128)(2,1)S(1)}, u32[]{:S(2)}, u32[]{:S(2)}) %collective-permute-start) | collective-permute-done | bytes 27680 | tf_op jit(solution)/shard_map/ppermute | solution.py:653
  43.4 0.6 %add_convert_fusion = bf16[6,2,1152]{2,1,0:T(2,128)(2,1)} fusion(f32[6,2,1152]{2,1,0:T(2,128)S(1)} %get-tuple-element.23, bf16[6,2,1152]{2,1,0:T(2,128)(2,1)S(1)} %collective-permute-done), kind=kLoop, calls=%fused_computation | loop fusion | flops 41472 | bytes 110592 | tf_op jit(solution)/shard_map/convert_element_type | solution.py:655
Async XLA Ops:
  0.6 38.4 %copy-start = (bf16[512,2304]{1,0:T(8,128)(2,1)S(1)}, bf16[512,2304]{1,0:T(8,128)(2,1)}, u32[]{:S(2)}) copy-start(bf16[512,2304]{1,0:T(8,128)(2,1)} %weight.3) | copy-start | bytes 7077892
  39.5 3.9 %collective-permute-start = (bf16[6,2,1152]{2,1,0:T(2,128)(2,1)S(1)}, bf16[6,2,1152]{2,1,0:T(2,128)(2,1)S(1)}, u32[]{:S(2)}, u32[]{:S(2)}) collective-permute-start(bf16[6,2,1152]{2,1,0:T(2,128)(2,1)S(1)} %get-tuple-element.24), channel_id=1, source_target_pairs={{0,1},{1,0},{2,3},{3,2},{4,5},{5,4},{6,7},{7,6},{8,9},{9,8},{10,11... | collective-permute-start | bytes 82952 | tf_op jit(solution)/shard_map/ppermute | solution.py:653

commit v9 on v8

--- a/solution.py
+++ b/solution.py
@@ -298,10 +298,7 @@
             total = frames[0] * weights[part][:1]
             for j in range(1, sz.taps + 1):
                 total = total + frames[j] * weights[part][j : j + 1]
-            below = 1.0 + jnp.exp(-total)
-            inverse = pltpu.reciprocal(below, approx=True)
-            inverse = inverse * (2.0 - below * inverse)
-            active.append(total * inverse)
+            active.append(total / (1.0 + jnp.exp(-total)))
             for tap in range(sz.taps):
                 window[tap][part] = jnp.where(alive, frames[tap + 1], frames[tap])
         retains.append(jnp.exp(-inputs[sz.parts]))

time: 44.3 us -> 44 us (level)
  no operation moved by 1% of the time
where the time goes in v9:
time: 44 us; the launch traced here: 43.7 us
  blocking collectives  34.7 us (79%)
  Pallas kernels  4.8 us (11%)
  starting transfers between devices  1.58 us (4%)
  waiting for transfers between devices  1.31 us (3%)
  between operations  0.67 us (2%)
  other arithmetic  0.64 us (1%)
    all_to_all x2, blocking collectives, exchange(): lax.all_to_all(pieces, 'rep', split_axis=0, concat_axis=0, axis_index_gro...  34.7 us
    pallas_call x1, Pallas kernels, local(): call(functools.partial(pack_kernel, sz), (shape((n, sz.state_rows + sz.in...  1.75 us
    pallas_call x1, Pallas kernels, local(): call(functools.partial(step_kernel, sz), (shape((n, sz.state_rows + sz.ba...  1.61 us
    ppermute x1, starting transfers between devices, local(): passed = lax.ppermute(partials[shift].astype(BF16), 'head', pairs)  1.58 us
    ppermute x1, waiting for transfers between devices, local(): passed = lax.ppermute(partials[shift].astype(BF16), 'head', pairs)  1.31 us
    pallas_call x1, Pallas kernels, local(): call(functools.partial(restore_kernel, sz, blocks), (shape(states.shape,...  1.03 us
  transfers between devices with their start and end apart: 1, of which 1 were waited for; matrix products, arithmetic and copies ran while one was open for 0% of the time, Pallas kernels for 2%

profile of v9, /device:TPU:0, one launch (start us, length us, event | category | flops | bytes accessed | tf_op | source)
XLA Modules:
  0.0 43.7 jit_solution(7353720016128095006)
XLA Ops:
  0.6 0.0 copy-start
  0.6 1.7 %pack.1 = (bf16[16,120,128]{2,1,0:T(8,128)(2,1)S(1)}, bf16[6,32,32]{2,1,0:T(8,128)(2,1)S(1)}, bf16[6,32,32]{2,1,0:T(8,128)(2,1)S(1)}, s32[8,32]{1,0:T(8,128)S(1)}, f32[3,4,128]{2,1,0:T(4,128)S(1)}) custom-call(s32[6,32]{1,0:T(8,128)} %refs_0_.1, s32[1,6]{1,0:T(1,128)} %bitcast.12, f32[1,4]{1,0:T(1,128)} %bitcast.14, f32[2,4,6]{2,1,0:T(4,128)} %bitcast.11, ...), custom_call_target="tpu_custom_call" | custom-call | tf_op jit(solution)/shard_map/pack/pallas_call | solution.py:571
  2.4 21.4 %all_to_all.10.came = bf16[16,120,128]{2,1,0:T(8,128)(2,1)S(1)} all-to-all(bf16[16,120,128]{2,1,0:T(8,128)(2,1)S(1)} %get-tuple-element.18), channel_id=1, replica_groups={{0,8,24,16,2,10,26,18,4,12,28,20,6,14,30,22},{1,9,25,17,3,11,27,19,5,13..., dimensions={0} | all-to-all | bytes 983040 | tf_op jit(solution)/shard_map/all_to_all | solution.py:534
  23.8 1.6 %steps.1 = (bf16[16,72,128]{2,1,0:T(8,128)(2,1)S(1)}, f32[16,512]{1,0:T(8,128)S(1)}) custom-call(f32[3,4,128]{2,1,0:T(4,128)S(1)} %get-tuple-element.15.filters, bf16[6,32,32]{2,1,0:T(8,128)(2,1)S(1)} %get-tuple-element.16.pick, bf16[6,32,32]{2,1,0:T(8,128)(2,1)S(1)} %get-tuple-element.17.place, bf16[16,120,128]{2,1,0:T(8,128)(2,1)S(1)} %all_to_all.10.came, ...), custom_call_target="tpu_custom_call" | custom-call | tf_op jit(solution)/shard_map/steps/pallas_call | solution.py:593
  25.4 13.3 %all_to_all.11.came = bf16[16,72,128]{2,1,0:T(8,128)(2,1)S(1)} all-to-all(bf16[16,72,128]{2,1,0:T(8,128)(2,1)S(1)} %get-tuple-element.21), channel_id=1, replica_groups={{0,8,24,16,2,10,26,18,4,12,28,20,6,14,30,22},{1,9,25,17,3,11,27,19,5,13..., dimensions={0} | all-to-all | bytes 589824 | tf_op jit(solution)/shard_map/all_to_all | solution.py:534
  38.7 0.0 copy-done
  38.7 0.4 project.1
  39.1 1.6 %collective-permute-start = (bf16[6,2,1152]{2,1,0:T(2,128)(2,1)S(1)}, bf16[6,2,1152]{2,1,0:T(2,128)(2,1)S(1)}, u32[]{:S(2)}, u32[]{:S(2)}) collective-permute-start(bf16[6,2,1152]{2,1,0:T(2,128)(2,1)S(1)} %get-tuple-element.24), channel_id=1, source_target_pairs={{0,1},{1,0},{2,3},{3,2},{4,5},{5,4},{6,7},{7,6},{8,9},{9,8},{10,11... | collective-permute-start | bytes 82952 | tf_op jit(solution)/shard_map/ppermute | solution.py:650
  40.7 1.0 %restore.1 = (f32[2,4,128,128]{3,2,1,0:T(8,128)}, f32[6,2,1152]{2,1,0:T(2,128)S(1)}, bf16[3,3,2,512]{3,2,1,0:T(2,128)(2,1)}) custom-call(bf16[16,512]{1,0:T(8,128)(2,1)S(1)} %get-tuple-element.22.gated, bf16[512,2304]{1,0:T(8,128)(2,1)S(1)} %copy-done, bf16[16,72,128]{2,1,0:T(8,128)(2,1)S(1)} %all_to_all.11.came), custom_call_target="tpu_custom_call" | custom-call | tf_op jit(solution)/shard_map/restore/pallas_call | solution.py:626
  41.8 1.3 %collective-permute-done = bf16[6,2,1152]{2,1,0:T(2,128)(2,1)S(1)} collective-permute-done((bf16[6,2,1152]{2,1,0:T(2,128)(2,1)S(1)}, bf16[6,2,1152]{2,1,0:T(2,128)(2,1)S(1)}, u32[]{:S(2)}, u32[]{:S(2)}) %collective-permute-start) | collective-permute-done | bytes 27680 | tf_op jit(solution)/shard_map/ppermute | solution.py:650
  43.1 0.6 %add_convert_fusion = bf16[6,2,1152]{2,1,0:T(2,128)(2,1)} fusion(f32[6,2,1152]{2,1,0:T(2,128)S(1)} %get-tuple-element.23, bf16[6,2,1152]{2,1,0:T(2,128)(2,1)S(1)} %collective-permute-done), kind=kLoop, calls=%fused_computation | loop fusion | flops 41472 | bytes 110592 | tf_op jit(solution)/shard_map/convert_element_type | solution.py:652
Async XLA Ops:
  0.6 38.1 %copy-start = (bf16[512,2304]{1,0:T(8,128)(2,1)S(1)}, bf16[512,2304]{1,0:T(8,128)(2,1)}, u32[]{:S(2)}) copy-start(bf16[512,2304]{1,0:T(8,128)(2,1)} %weight.3) | copy-start | bytes 7077892
  39.1 3.9 %collective-permute-start = (bf16[6,2,1152]{2,1,0:T(2,128)(2,1)S(1)}, bf16[6,2,1152]{2,1,0:T(2,128)(2,1)S(1)}, u32[]{:S(2)}, u32[]{:S(2)}) collective-permute-start(bf16[6,2,1152]{2,1,0:T(2,128)(2,1)S(1)} %get-tuple-element.24), channel_id=1, source_target_pairs={{0,1},{1,0},{2,3},{3,2},{4,5},{5,4},{6,7},{7,6},{8,9},{9,8},{10,11... | collective-permute-start | bytes 82952 | tf_op jit(solution)/shard_map/ppermute | solution.py:650

commit v10 on v9

--- a/solution.py
+++ b/solution.py
@@ -257,7 +257,7 @@
 def step_kernel(sz, filters, pick, place, came, *refs):
     count = sz.groups
     sources, sent, factor, scratch = refs[:4], refs[4], refs[5], refs[6:]
-    scalars, live, gain, gate, info, later, back, sems = scratch
+    scalars, live, gain, gate, info, parked, later, back, sems = scratch
     copies = []
     for i, (source, target) in enumerate(zip(sources, scratch)):
         copies.append(pltpu.make_async_copy(source, target, sems.at[i]))
@@ -338,9 +338,6 @@
     for value in values:
         value = over_blocks(sz, jnp.where(own_lanes, value, 0.0))
         value_cols.append(jnp.concatenate([value] * wide, axis=1))
-    for copy in copies:
-        copy.wait()
-    gate_factor(sz, live, gain, gate, factor)
     lane_row = quotient(iota((sz.tile, sz.width), 1), sz.cols)
     own = iota((sz.tile, sz.width), 0) == lane_row
     readouts = [[] for _ in range(T)]
@@ -385,12 +382,7 @@
         for i in range(sz.tile):
             part = block[i].astype(F32) * reach[at + i : at + i + 1]
             part = part + added[i * sz.cols : (i + 1) * sz.cols]
-            to = scalars[0, at + i]
-            if sz.whole_tiles:
-                start = pl.multiple_of(mod(to, sz.rows) * sz.cols, sz.cols)
-                sent[quotient(to, sz.rows), pl.ds(start, sz.cols), :] = part.astype(BF16)
-            else:
-                later[pl.ds(pl.multiple_of(to * sz.cols, sz.cols), sz.cols), :] = part
+            parked[at + i] = part.astype(parked.dtype)
     blocks = [in_block(sz, (n, dk), cut, shift) for shift in range(4)]
     placed = [None] * sz.back_depth
     kept = [None] * sz.back_depth
@@ -417,6 +409,16 @@
         if placed[slot] is not None:
             value = value + placed[slot]
         back[pl.ds(slot, n, stride=sz.back_depth), :] = value
+    for copy in copies:
+        copy.wait()
+    gate_factor(sz, live, gain, gate, factor)
+    for at in range(n):
+        to = scalars[0, at]
+        if sz.whole_tiles:
+            start_row = pl.multiple_of(mod(to, sz.rows) * sz.cols, sz.cols)
+            sent[quotient(to, sz.rows), pl.ds(start_row, sz.cols), :] = parked[at]
+        else:
+            later[pl.ds(pl.multiple_of(to * sz.cols, sz.cols), sz.cols), :] = parked[at]
     for g in range(count):
         p = sz.place_of[g]
         if not sz.whole_tiles:
@@ -604,6 +606,7 @@
             pltpu.VMEM(gain.shape, F32),
             pltpu.VMEM(out_gate.shape, BF16),
             pltpu.VMEM((n * sz.info_rows, sz.dk), F32),
+            pltpu.VMEM((sz.slots, sz.cols, sz.dk), BF16 if sz.whole_tiles else F32),
             pltpu.VMEM((8 if sz.whole_tiles else n * sz.state_rows, sz.dk), F32),
             pltpu.VMEM((n * sz.back_rows, sz.dk), F32),
             pltpu.SemaphoreType.DMA((4,)),

time: 44 us -> 43.9 us (level)
  no operation moved by 1% of the time
where the time goes in v10:
time: 43.9 us; the launch traced here: 43.7 us
  blocking collectives  34.7 us (79%)
  Pallas kernels  4.75 us (11%)
  starting transfers between devices  1.58 us (4%)
  waiting for transfers between devices  1.31 us (3%)
  between operations  0.67 us (2%)
  other arithmetic  0.64 us (1%)
    all_to_all x2, blocking collectives, exchange(): lax.all_to_all(pieces, 'rep', split_axis=0, concat_axis=0, axis_index_gro...  34.7 us
    pallas_call x1, Pallas kernels, local(): call(functools.partial(pack_kernel, sz), (shape((n, sz.state_rows + sz.in...  1.75 us
    ppermute x1, starting transfers between devices, local(): passed = lax.ppermute(partials[shift].astype(BF16), 'head', pairs)  1.58 us
    pallas_call x1, Pallas kernels, local(): call(functools.partial(step_kernel, sz), (shape((n, sz.state_rows + sz.ba...  1.57 us
    ppermute x1, waiting for transfers between devices, local(): passed = lax.ppermute(partials[shift].astype(BF16), 'head', pairs)  1.31 us
    pallas_call x1, Pallas kernels, local(): call(functools.partial(restore_kernel, sz, blocks), (shape(states.shape,...  1.03 us
  transfers between devices with their start and end apart: 1, of which 1 were waited for; matrix products, arithmetic and copies ran while one was open for 0% of the time, Pallas kernels for 2%

profile of v10, /device:TPU:0, one launch (start us, length us, event | category | flops | bytes accessed | tf_op | source)
XLA Modules:
  0.0 43.7 jit_solution(12815790716158364138)
XLA Ops:
  0.6 0.0 copy-start
  0.6 1.7 %pack.1 = (bf16[16,120,128]{2,1,0:T(8,128)(2,1)S(1)}, bf16[6,32,32]{2,1,0:T(8,128)(2,1)S(1)}, bf16[6,32,32]{2,1,0:T(8,128)(2,1)S(1)}, s32[8,32]{1,0:T(8,128)S(1)}, f32[3,4,128]{2,1,0:T(4,128)S(1)}) custom-call(s32[6,32]{1,0:T(8,128)} %refs_0_.1, s32[1,6]{1,0:T(1,128)} %bitcast.12, f32[1,4]{1,0:T(1,128)} %bitcast.14, f32[2,4,6]{2,1,0:T(4,128)} %bitcast.11, ...), custom_call_target="tpu_custom_call" | custom-call | tf_op jit(solution)/shard_map/pack/pallas_call | solution.py:573
  2.4 21.4 %all_to_all.10.came = bf16[16,120,128]{2,1,0:T(8,128)(2,1)S(1)} all-to-all(bf16[16,120,128]{2,1,0:T(8,128)(2,1)S(1)} %get-tuple-element.18), channel_id=1, replica_groups={{0,8,24,16,2,10,26,18,4,12,28,20,6,14,30,22},{1,9,25,17,3,11,27,19,5,13..., dimensions={0} | all-to-all | bytes 983040 | tf_op jit(solution)/shard_map/all_to_all | solution.py:536
  23.8 1.6 %steps.1 = (bf16[16,72,128]{2,1,0:T(8,128)(2,1)S(1)}, f32[16,512]{1,0:T(8,128)S(1)}) custom-call(f32[3,4,128]{2,1,0:T(4,128)S(1)} %get-tuple-element.15.filters, bf16[6,32,32]{2,1,0:T(8,128)(2,1)S(1)} %get-tuple-element.16.pick, bf16[6,32,32]{2,1,0:T(8,128)(2,1)S(1)} %get-tuple-element.17.place, bf16[16,120,128]{2,1,0:T(8,128)(2,1)S(1)} %all_to_all.10.came, ...), custom_call_target="tpu_custom_call" | custom-call | tf_op jit(solution)/shard_map/steps/pallas_call | solution.py:595
  25.4 13.3 %all_to_all.11.came = bf16[16,72,128]{2,1,0:T(8,128)(2,1)S(1)} all-to-all(bf16[16,72,128]{2,1,0:T(8,128)(2,1)S(1)} %get-tuple-element.21), channel_id=1, replica_groups={{0,8,24,16,2,10,26,18,4,12,28,20,6,14,30,22},{1,9,25,17,3,11,27,19,5,13..., dimensions={0} | all-to-all | bytes 589824 | tf_op jit(solution)/shard_map/all_to_all | solution.py:536
  38.7 0.0 copy-done
  38.7 0.4 project.1
  39.1 1.6 %collective-permute-start = (bf16[6,2,1152]{2,1,0:T(2,128)(2,1)S(1)}, bf16[6,2,1152]{2,1,0:T(2,128)(2,1)S(1)}, u32[]{:S(2)}, u32[]{:S(2)}) collective-permute-start(bf16[6,2,1152]{2,1,0:T(2,128)(2,1)S(1)} %get-tuple-element.24), channel_id=1, source_target_pairs={{0,1},{1,0},{2,3},{3,2},{4,5},{5,4},{6,7},{7,6},{8,9},{9,8},{10,11... | collective-permute-start | bytes 82952 | tf_op jit(solution)/shard_map/ppermute | solution.py:653
  40.7 1.0 %restore.1 = (f32[2,4,128,128]{3,2,1,0:T(8,128)}, f32[6,2,1152]{2,1,0:T(2,128)S(1)}, bf16[3,3,2,512]{3,2,1,0:T(2,128)(2,1)}) custom-call(bf16[16,512]{1,0:T(8,128)(2,1)S(1)} %get-tuple-element.22.gated, bf16[512,2304]{1,0:T(8,128)(2,1)S(1)} %copy-done, bf16[16,72,128]{2,1,0:T(8,128)(2,1)S(1)} %all_to_all.11.came), custom_call_target="tpu_custom_call" | custom-call | tf_op jit(solution)/shard_map/restore/pallas_call | solution.py:629
  41.7 1.3 %collective-permute-done = bf16[6,2,1152]{2,1,0:T(2,128)(2,1)S(1)} collective-permute-done((bf16[6,2,1152]{2,1,0:T(2,128)(2,1)S(1)}, bf16[6,2,1152]{2,1,0:T(2,128)(2,1)S(1)}, u32[]{:S(2)}, u32[]{:S(2)}) %collective-permute-start) | collective-permute-done | bytes 27680 | tf_op jit(solution)/shard_map/ppermute | solution.py:653
  43.0 0.6 %add_convert_fusion = bf16[6,2,1152]{2,1,0:T(2,128)(2,1)} fusion(f32[6,2,1152]{2,1,0:T(2,128)S(1)} %get-tuple-element.23, bf16[6,2,1152]{2,1,0:T(2,128)(2,1)S(1)} %collective-permute-done), kind=kLoop, calls=%fused_computation | loop fusion | flops 41472 | bytes 110592 | tf_op jit(solution)/shard_map/convert_element_type | solution.py:655
Async XLA Ops:
  0.6 38.0 %copy-start = (bf16[512,2304]{1,0:T(8,128)(2,1)S(1)}, bf16[512,2304]{1,0:T(8,128)(2,1)}, u32[]{:S(2)}) copy-start(bf16[512,2304]{1,0:T(8,128)(2,1)} %weight.3) | copy-start | bytes 7077892
  39.1 3.9 %collective-permute-start = (bf16[6,2,1152]{2,1,0:T(2,128)(2,1)S(1)}, bf16[6,2,1152]{2,1,0:T(2,128)(2,1)S(1)}, u32[]{:S(2)}, u32[]{:S(2)}) collective-permute-start(bf16[6,2,1152]{2,1,0:T(2,128)(2,1)S(1)} %get-tuple-element.24), channel_id=1, source_target_pairs={{0,1},{1,0},{2,3},{3,2},{4,5},{5,4},{6,7},{7,6},{8,9},{9,8},{10,11... | collective-permute-start | bytes 82952 | tf_op jit(solution)/shard_map/ppermute | solution.py:653

commit v11 on v10

--- a/solution.py
+++ b/solution.py
@@ -557,6 +557,7 @@
     sz = Sizes(group_total, states, conv_states, projected)
     n, channels = sz.groups, sz.heads * sz.dk
     shape = jax.ShapeDtypeStruct
+    spare_info = round_up(sz.info_rows + sz.info_sets, 8)
     lives = live_counts.T
     arguments = (
         destinations,
@@ -583,8 +584,8 @@
         (vmem(),) * 5,
         [pltpu.VMEM(x.shape, x.dtype) for x in arguments]
         + [
-            pltpu.VMEM((sz.heads, sz.info_rows, sz.dk), F32),
-            pltpu.VMEM((3, sz.heads, sz.info_rows, sz.dk), F32),
+            pltpu.VMEM((sz.heads, spare_info, sz.dk), F32),
+            pltpu.VMEM((3, sz.heads, spare_info, sz.dk), F32),
             pltpu.VMEM((sz.heads, sz.dk), F32),
             pltpu.SemaphoreType.DMA((len(arguments),)),
         ],
@@ -605,10 +606,10 @@
             pltpu.VMEM(lives.shape, lives.dtype),
             pltpu.VMEM(gain.shape, F32),
             pltpu.VMEM(out_gate.shape, BF16),
-            pltpu.VMEM((n * sz.info_rows, sz.dk), F32),
+            pltpu.VMEM((round_up(n * sz.info_rows + sz.info_sets, 8), sz.dk), F32),
             pltpu.VMEM((sz.slots, sz.cols, sz.dk), BF16 if sz.whole_tiles else F32),
             pltpu.VMEM((8 if sz.whole_tiles else n * sz.state_rows, sz.dk), F32),
-            pltpu.VMEM((n * sz.back_rows, sz.dk), F32),
+            pltpu.VMEM((round_up(n * sz.back_rows + sz.back_depth, 8), sz.dk), F32),
             pltpu.SemaphoreType.DMA((4,)),
         ],
         "steps",

time: 43.9 us -> 43.9 us (level)
  no operation moved by 1% of the time
where the time goes in v11:
time: 43.9 us; the launch traced here: 43.7 us
  blocking collectives  34.7 us (79%)
  Pallas kernels  4.75 us (11%)
  starting transfers between devices  1.58 us (4%)
  waiting for transfers between devices  1.31 us (3%)
  between operations  0.67 us (2%)
  other arithmetic  0.64 us (1%)
    all_to_all x2, blocking collectives, exchange(): lax.all_to_all(pieces, 'rep', split_axis=0, concat_axis=0, axis_index_gro...  34.7 us
    pallas_call x1, Pallas kernels, local(): call(functools.partial(pack_kernel, sz), (shape((n, sz.state_rows + sz.in...  1.75 us
    ppermute x1, starting transfers between devices, local(): passed = lax.ppermute(partials[shift].astype(BF16), 'head', pairs)  1.58 us
    pallas_call x1, Pallas kernels, local(): call(functools.partial(step_kernel, sz), (shape((n, sz.state_rows + sz.ba...  1.57 us
    ppermute x1, waiting for transfers between devices, local(): passed = lax.ppermute(partials[shift].astype(BF16), 'head', pairs)  1.31 us
    pallas_call x1, Pallas kernels, local(): call(functools.partial(restore_kernel, sz, blocks), (shape(states.shape,...  1.03 us
  transfers between devices with their start and end apart: 1, of which 1 were waited for; matrix products, arithmetic and copies ran while one was open for 0% of the time, Pallas kernels for 2%

profile of v11, /device:TPU:0, one launch (start us, length us, event | category | flops | bytes accessed | tf_op | source)
XLA Modules:
  0.0 43.7 jit_solution(12429029182848841908)
XLA Ops:
  0.6 0.0 copy-start
  0.6 1.7 %pack.1 = (bf16[16,120,128]{2,1,0:T(8,128)(2,1)S(1)}, bf16[6,32,32]{2,1,0:T(8,128)(2,1)S(1)}, bf16[6,32,32]{2,1,0:T(8,128)(2,1)S(1)}, s32[8,32]{1,0:T(8,128)S(1)}, f32[3,4,128]{2,1,0:T(4,128)S(1)}) custom-call(s32[6,32]{1,0:T(8,128)} %refs_0_.1, s32[1,6]{1,0:T(1,128)} %bitcast.12, f32[1,4]{1,0:T(1,128)} %bitcast.14, f32[2,4,6]{2,1,0:T(4,128)} %bitcast.11, ...), custom_call_target="tpu_custom_call" | custom-call | tf_op jit(solution)/shard_map/pack/pallas_call | solution.py:574
  2.4 21.4 %all_to_all.10.came = bf16[16,120,128]{2,1,0:T(8,128)(2,1)S(1)} all-to-all(bf16[16,120,128]{2,1,0:T(8,128)(2,1)S(1)} %get-tuple-element.18), channel_id=1, replica_groups={{0,8,24,16,2,10,26,18,4,12,28,20,6,14,30,22},{1,9,25,17,3,11,27,19,5,13..., dimensions={0} | all-to-all | bytes 983040 | tf_op jit(solution)/shard_map/all_to_all | solution.py:536
  23.8 1.6 %steps.1 = (bf16[16,72,128]{2,1,0:T(8,128)(2,1)S(1)}, f32[16,512]{1,0:T(8,128)S(1)}) custom-call(f32[3,4,128]{2,1,0:T(4,128)S(1)} %get-tuple-element.15.filters, bf16[6,32,32]{2,1,0:T(8,128)(2,1)S(1)} %get-tuple-element.16.pick, bf16[6,32,32]{2,1,0:T(8,128)(2,1)S(1)} %get-tuple-element.17.place, bf16[16,120,128]{2,1,0:T(8,128)(2,1)S(1)} %all_to_all.10.came, ...), custom_call_target="tpu_custom_call" | custom-call | tf_op jit(solution)/shard_map/steps/pallas_call | solution.py:596
  25.4 13.3 %all_to_all.11.came = bf16[16,72,128]{2,1,0:T(8,128)(2,1)S(1)} all-to-all(bf16[16,72,128]{2,1,0:T(8,128)(2,1)S(1)} %get-tuple-element.21), channel_id=1, replica_groups={{0,8,24,16,2,10,26,18,4,12,28,20,6,14,30,22},{1,9,25,17,3,11,27,19,5,13..., dimensions={0} | all-to-all | bytes 589824 | tf_op jit(solution)/shard_map/all_to_all | solution.py:536
  38.7 0.0 copy-done
  38.7 0.4 project.1
  39.1 1.6 %collective-permute-start = (bf16[6,2,1152]{2,1,0:T(2,128)(2,1)S(1)}, bf16[6,2,1152]{2,1,0:T(2,128)(2,1)S(1)}, u32[]{:S(2)}, u32[]{:S(2)}) collective-permute-start(bf16[6,2,1152]{2,1,0:T(2,128)(2,1)S(1)} %get-tuple-element.24), channel_id=1, source_target_pairs={{0,1},{1,0},{2,3},{3,2},{4,5},{5,4},{6,7},{7,6},{8,9},{9,8},{10,11... | collective-permute-start | bytes 82952 | tf_op jit(solution)/shard_map/ppermute | solution.py:654
  40.7 1.0 %restore.1 = (f32[2,4,128,128]{3,2,1,0:T(8,128)}, f32[6,2,1152]{2,1,0:T(2,128)S(1)}, bf16[3,3,2,512]{3,2,1,0:T(2,128)(2,1)}) custom-call(bf16[16,512]{1,0:T(8,128)(2,1)S(1)} %get-tuple-element.22.gated, bf16[512,2304]{1,0:T(8,128)(2,1)S(1)} %copy-done, bf16[16,72,128]{2,1,0:T(8,128)(2,1)S(1)} %all_to_all.11.came), custom_call_target="tpu_custom_call" | custom-call | tf_op jit(solution)/shard_map/restore/pallas_call | solution.py:630
  41.7 1.3 %collective-permute-done = bf16[6,2,1152]{2,1,0:T(2,128)(2,1)S(1)} collective-permute-done((bf16[6,2,1152]{2,1,0:T(2,128)(2,1)S(1)}, bf16[6,2,1152]{2,1,0:T(2,128)(2,1)S(1)}, u32[]{:S(2)}, u32[]{:S(2)}) %collective-permute-start) | collective-permute-done | bytes 27680 | tf_op jit(solution)/shard_map/ppermute | solution.py:654
  43.0 0.6 %add_convert_fusion = bf16[6,2,1152]{2,1,0:T(2,128)(2,1)} fusion(f32[6,2,1152]{2,1,0:T(2,128)S(1)} %get-tuple-element.23, bf16[6,2,1152]{2,1,0:T(2,128)(2,1)S(1)} %collective-permute-done), kind=kLoop, calls=%fused_computation | loop fusion | flops 41472 | bytes 110592 | tf_op jit(solution)/shard_map/convert_element_type | solution.py:656
Async XLA Ops:
  0.6 38.0 %copy-start = (bf16[512,2304]{1,0:T(8,128)(2,1)S(1)}, bf16[512,2304]{1,0:T(8,128)(2,1)}, u32[]{:S(2)}) copy-start(bf16[512,2304]{1,0:T(8,128)(2,1)} %weight.3) | copy-start | bytes 7077892
  39.1 3.9 %collective-permute-start = (bf16[6,2,1152]{2,1,0:T(2,128)(2,1)S(1)}, bf16[6,2,1152]{2,1,0:T(2,128)(2,1)S(1)}, u32[]{:S(2)}, u32[]{:S(2)}) collective-permute-start(bf16[6,2,1152]{2,1,0:T(2,128)(2,1)S(1)} %get-tuple-element.24), channel_id=1, source_target_pairs={{0,1},{1,0},{2,3},{3,2},{4,5},{5,4},{6,7},{7,6},{8,9},{9,8},{10,11... | collective-permute-start | bytes 82952 | tf_op jit(solution)/shard_map/ppermute | solution.py:654
